TPU v7x, 256 devices: a whole 4x4x8 slice. The times are simulated.
256 devices in a mesh: noise: 8 (over x, core), region: 32 (over z, y).
Axes of the slice: x: 4, y: 4, z: 8, core: 2. Of those that a mesh axis runs over, the one named last changes fastest.
Arguments:
- target_state: bfloat16 [84, 65536], P(None, 'region'), may hold values from -6 to 6
- noise_field: bfloat16 [8, 84, 65536], P('noise', None, 'region'), may hold values from -6 to 6
- level_index: int32 [8], P('noise'), may hold values from 0 to 19
- send_rows: int32 [32, 32, 128], P('region'), may hold values from 0 to 2047, as said below
- edge_src: int32 [131072], P('region'), may hold values from 0 to 4095, as said below
- edge_dst: int32 [131072], P('region'), may hold values from 0 to 256, as said below
- edge_geom: bfloat16 [4, 131072], P(None, 'region'), may hold values from -1 to 1
- mesh_init: bfloat16 [8192, 512], P('region'), may hold values from -6 to 6
- neighbours: int32 [8192, 32], P('region'), may hold values from 0 to 8191, as said below
- grid_weight: bfloat16 [84, 512], replicated, may hold values from -0.625 to 0.625
- edge_weight: bfloat16 [4, 512], replicated, may hold values from -3 to 3
- message_weight: bfloat16 [512, 512], replicated, may hold values from -0.25 to 0.25
- enc_gain: float32 [512], replicated, may hold values from 0.5 to 1.5
- att_gain: float32 [512], replicated, may hold values from 0.5 to 1.5
- qkv_weight: bfloat16 [512, 1536], replicated, may hold values from -0.25 to 0.25
- out_weight: bfloat16 [512, 512], replicated, may hold values from -0.25 to 0.25
- cotangent: bfloat16 [8, 8192, 512], P('noise', 'region'), may hold values from -0.1875 to 0.1875
Outputs:
- mesh_out: bfloat16 [8, 8192, 512], P('noise', 'region')
- out_grad: float32 [512, 512], replicated
Inputs may be any that keep to these rules, and one draw needn't show every extreme that they name: `send_rows`: for band b and region r a leading run of slots, of at least a quarter of 128, holds rows to be sent; the other slots hold 0. In some region every band fills all 128 slots. `edge_src`: only live slots are named: s is below the length of the leading run that band b sends to the edge's region. Padding slots hold 0. In each region the live edge slots come first, a multiple of 128 of them and at least a quarter of 4096; some region fills all of them. The rest are padding with edge_dst 256. `neighbours`: A neighbour of node r * 256 + i has the index r * 256 + i + o modulo 8192, with o between -128 and 128.
All inputs are finite; a program needn't handle non-finite values.
Results may differ from a plain program's by a relative error of at most 0.0065.
Values may be sent and summed in bfloat16 or wider, within the bound.
A program may use at most 64 MiB of HBM per device.

v0:
```python
import math

import jax
import jax.numpy as jnp
from jax import lax
from jax.sharding import PartitionSpec as P

HEADS = 4
PLAN = 20
HALO = 128


sigma_max = 80.0
sigma_min = 0.03
plan_rho = 7.0
norm_eps = 1e-05
head_eps = 1e-06


def extended(array, sides, width):
    for axis, dim in sides:
        peers, length = (lax.axis_size(axis), array.shape[dim])
        up = [(i, (i + 1) % peers) for i in range(peers)]
        down = [(j, i) for i, j in up]
        last = lax.slice_in_dim(array, length - width, length, axis=dim)
        leading = lax.slice_in_dim(array, 0, width, axis=dim)
        before = lax.ppermute(last, axis, up)
        after = lax.ppermute(leading, axis, down)
        array = jnp.concatenate([before, array, after], axis=dim)
    return array


def noise_level(index):
    upper_root = sigma_max ** (1.0 / plan_rho)
    lower_root = sigma_min ** (1.0 / plan_rho)
    fraction = index.astype(jnp.float32) / (PLAN - 1)
    return (upper_root + fraction * (lower_root - upper_root)) ** plan_rho


def rms_scale(values, gain, epsilon):
    return values * lax.rsqrt(jnp.mean(values * values, axis=-1, keepdims=True) + epsilon) * gain


def head_unit(values, head_size):
    shaped = values.reshape(values.shape[0], HEADS, head_size)
    return (
        shaped * lax.rsqrt(jnp.mean(shaped * shaped, axis=-1, keepdims=True) + head_eps)
    ).astype(jnp.bfloat16)


def body(
    target_state,
    noise_field,
    level_index,
    send_rows,
    edge_src,
    edge_dst,
    edge_geom,
    mesh_init,
    neighbours,
    grid_weight,
    edge_weight,
    message_weight,
    enc_gain,
    att_gain,
    qkv_weight,
    out_weight,
    cotangent,
):
    contract = (((0,), (0,)), ((), ()))
    regions = lax.axis_size("region")
    region_pos = lax.axis_index("region")
    nodes = mesh_init.shape[0]
    width = mesh_init.shape[1]
    head_size = width // HEADS
    slots = send_rows.shape[2]
    send_list = send_rows.reshape(-1)
    edge_terms = lax.dot_general(
        edge_geom, edge_weight, contract, preferred_element_type=jnp.float32
    )
    node_table = (jnp.arange(nodes, dtype=jnp.int32)[:, None] == edge_dst[None, :]).astype(
        jnp.bfloat16
    )
    message_full = message_weight.astype(jnp.float32)
    local_index = (neighbours - region_pos * nodes + HALO) % (nodes * regions)
    block_rows = 128
    block_count = nodes // block_rows
    index_blocks = local_index.reshape(block_count, block_rows, local_index.shape[1])
    mesh_base = mesh_init.astype(jnp.float32)
    sigma_level = noise_level(level_index[0])
    grid_in = (
        (target_state.astype(jnp.float32) + sigma_level * noise_field[0].astype(jnp.float32))
        / jnp.sqrt(1.0 + sigma_level * sigma_level)
    ).astype(jnp.bfloat16)
    picked = jnp.take(grid_in, send_list, axis=1)
    embedded = lax.dot_general(
        picked, grid_weight, contract, preferred_element_type=jnp.float32
    ).astype(jnp.bfloat16)
    incoming = lax.all_to_all(
        embedded.reshape(regions, slots, width), "region", split_axis=0, concat_axis=0, tiled=True
    )
    row_table = incoming.reshape(regions * slots, width)
    source_rows = jnp.take(row_table, edge_src, axis=0)
    hidden = jax.nn.silu(source_rows.astype(jnp.float32) + edge_terms).astype(jnp.bfloat16)
    hidden_sum = jnp.dot(node_table, hidden, preferred_element_type=jnp.float32)
    aggregate = jnp.dot(hidden_sum, message_full, precision=lax.Precision.HIGHEST)
    encoded = mesh_base + rms_scale(aggregate, enc_gain, norm_eps)
    normed = rms_scale(encoded, att_gain, norm_eps).astype(jnp.bfloat16)
    projected = jnp.dot(normed, qkv_weight, preferred_element_type=jnp.float32)
    query_unit = head_unit(projected[:, :width], head_size)
    key_unit = head_unit(projected[:, width : 2 * width], head_size)
    value_part = projected[:, 2 * width :].astype(jnp.bfloat16)
    key_values = jnp.concatenate([key_unit.reshape(nodes, width), value_part], axis=1)
    padded = extended(key_values, (("region", 0),), HALO)

    def attend(inputs):
        queries, index_block = inputs
        nearby = jnp.take(padded, index_block, axis=0)
        keys_near = nearby[:, :, :width].reshape(block_rows, index_block.shape[1], HEADS, head_size)
        values_near = nearby[:, :, width:].reshape(
            block_rows, index_block.shape[1], HEADS, head_size
        )
        scores = jnp.einsum(
            "bhd,bkhd->bhk", queries, keys_near, preferred_element_type=jnp.float32
        ) / math.sqrt(head_size)
        weights = jnp.exp(scores)
        weights = (weights / jnp.sum(weights, axis=-1, keepdims=True)).astype(jnp.bfloat16)
        mixed = jnp.einsum(
            "bhk,bkhd->bhd", weights, values_near, preferred_element_type=jnp.float32
        )
        return mixed.reshape(block_rows, width).astype(jnp.bfloat16)

    attended = lax.map(
        attend, (query_unit.reshape(block_count, block_rows, HEADS, head_size), index_blocks)
    ).reshape(nodes, width)
    level_states = [
        (encoded + jnp.dot(attended, out_weight, preferred_element_type=jnp.float32)).astype(
            jnp.bfloat16
        )
    ]
    partial_value = lax.dot_general(
        attended, cotangent[0], contract, preferred_element_type=jnp.float32
    )
    out_grad = lax.psum(partial_value, ("noise", "region"))
    return (jnp.stack(level_states), out_grad)


def solution(mesh):
    in_specs = (
        P(None, "region"),
        P("noise", None, "region"),
        P("noise"),
        P("region", None, None),
        P("region"),
        P("region"),
        P(None, "region"),
        P("region", None),
        P("region", None),
        P(),
        P(),
        P(),
        P(),
        P(),
        P(),
        P(),
        P("noise", "region", None),
    )
    out_specs = (P("noise", "region", None), P())
    return jax.shard_map(body, mesh=mesh, in_specs=in_specs, out_specs=out_specs, check_vma=False)
```

profile of v0, /device:TPU:1, one launch (start us, length us, event | category | flops | bytes accessed | tf_op | source)
XLA Modules:
  0.0 520.1 jit_solution(9854553082815629282)
XLA Ops:
  8.0 1.3 copy.33
  9.3 1.3 copy.34
  12.3 12.1 %gather_fusion.1 = bf16[4096,84]{1,0:T(8,128)(2,1)S(1)} fusion(bf16[84,2048]{0,1:T(8,128)(2,1)S(1)} %fusion.21, s32[4096]{0:T(1024)S(1)} %broadcast_clamp_fusion.1), kind=kCustom, calls=%fused_computation.1 | custom fusion | bytes 1392640 | tf_op jit(solution)/shard_map/jit(_take)/gather | solution.py:95
  24.5 2.9 convolution_convert_fusion
  27.4 12.3 %all-to-all-start = ((bf16[32,128,512]{2,1,0:T(8,128)(2,1)}), bf16[32,128,512]{2,1,0:T(8,128)(2,1)}, u32[]{:S(2)}, u32[]{:S(2)}) async-start(bf16[32,128,512]{2,1,0:T(8,128)(2,1)} %bitcast.94), calls=%async_computation | async-start | bytes 8388608 | tf_op jit(solution)/shard_map/all_to_all | solution.py:99
  39.9 92.8 %all-to-all-done = bf16[32,128,512]{2,1,0:T(8,128)(2,1)} async-done(((bf16[32,128,512]{2,1,0:T(8,128)(2,1)}), bf16[32,128,512]{2,1,0:T(8,128)(2,1)}, u32[]{:S(2)}, u32[]{:S(2)}) %all-to-all-start) | async-done | bytes 4194336 | tf_op jit(solution)/shard_map/all_to_all | solution.py:99
  132.7 20.1 %gather_fusion.2 = bf16[4096,512]{1,0:T(8,128)(2,1)} fusion(bf16[4096,512]{1,0:T(8,128)(2,1)} %bitcast.15, s32[4096]{0:T(1024)S(1)} %fusion.33), kind=kCustom, calls=%fused_computation.2 | custom fusion | bytes 8404992 | tf_op jit(solution)/shard_map/jit(_take)/gather | solution.py:103
  152.9 6.3 %fusion.16 = f32[256,512]{1,0:T(8,128)S(1)} fusion(s32[4096]{0:T(1024)S(1)} %copy-done.17, bf16[4,4096]{1,0:T(4,128)(2,1)S(1)} %copy-done.16, bf16[4,512]{1,0:T(4,128)(2,1)S(1)} %copy-done.18, bf16[4096,512]{1,0:T(8,128)(2,1)} %gather_fusion.2, pred[4096]{0:T(1024)(128)(4,1)S(1)} %compare_and_fusion.2), kind=kOutput, calls=%fused_computation.31 | convolution fusion | flops 1108344832 | bytes 4775936 | tf_op jit(solution)/shard_map/dot_general | solution.py:105
  162.3 2.0 mul.115
  164.3 2.0 reduce_sum.48
  169.5 2.6 collective-permute-start
  172.1 2.3 collective-permute-start.1
  174.4 1.2 mul.110
  176.0 1.2 reshape.180
  179.2 1.2 pad_maximum_fusion
  180.4 71.9 %while.10 = (s32[]{:T(128)}, bf16[2,128,512]{2,1,0:T(8,128)(2,1)}, bf16[2,128,4,128]{3,2,1,0:T(4,128)(2,1)}, s32[2,128,32]{2,1,0:T(8,128)S(1)}, bf16[512,1024]{1,0:T(8,128)(2,1)S(1)}, /*index=5*/s32[]{:T(128)}) while((s32[]{:T(128)}, bf16[2,128,512]{2,1,0:T(8,128)(2,1)}, bf16[2,128,4,128]{3,2,1,0:T(4,128)(2,1)}, s32[2,128,32]{2,1,0:T(8,128)S(1)}, ...), condition=%wide.region_6.7_spmd, body=%wide.region_4.6_spmd.sunk | while | flops 12739105 | bytes 61874796 | solution.py:133
  180.5 18.2 %gather_fusion = bf16[4096,1024]{1,0:T(8,128)(2,1)} fusion(bf16[512,1024]{1,0:T(8,128)(2,1)S(1)} %get-tuple-element.100, s32[4096]{0:T(1024)S(1)} %broadcast_clamp_fusion.3), kind=kCustom, calls=%fused_computation.clone.1 | custom fusion | bytes 16793600 | tf_op jit(solution)/shard_map/while/body/eval_jaxpr/jit(_take)/gather | solution.py:118
  198.8 4.5 broadcast_select_fusion.2
  203.3 3.4 slice_bitcast_fusion.3
  206.8 2.3 fusion.60
  209.8 1.5 fusion.61
  212.2 3.4 fusion.62
  216.5 18.2 %gather_fusion = bf16[4096,1024]{1,0:T(8,128)(2,1)} fusion(bf16[512,1024]{1,0:T(8,128)(2,1)S(1)} %get-tuple-element.100, s32[4096]{0:T(1024)S(1)} %broadcast_clamp_fusion.3), kind=kCustom, calls=%fused_computation.clone.1 | custom fusion | bytes 16793600 | tf_op jit(solution)/shard_map/while/body/eval_jaxpr/jit(_take)/gather | solution.py:118
  234.8 4.5 broadcast_select_fusion.2
  239.3 3.4 slice_bitcast_fusion.3
  242.8 2.3 fusion.60
  245.8 1.5 fusion.61
  248.2 3.4 fusion.62
  252.4 2.3 fusion.28
  254.7 2.2 fusion.19
  256.9 254.0 %all-reduce.2.cloned.1.call-done = f32[512,512]{1,0:T(8,128)} async-done(((f32[512,512]{1,0:T(8,128)}), f32[512,512]{1,0:T(8,128)}) %all-reduce.2.cloned.1.call-update) | async-done | bytes 1048592 | tf_op jit(solution)/shard_map/psum | solution.py:144
  510.9 2.3 copy.84
  (87 shorter events, 15.7 us)
Async XLA Ops:
  7.2 153.6 %copy-start = (bf16[512,1536]{1,0:T(8,128)(2,1)S(1)}, bf16[512,1536]{1,0:T(8,128)(2,1)}, u32[]{:S(2)}) copy-start(bf16[512,1536]{1,0:T(8,128)(2,1)} %param.33) | copy-start | bytes 4718596
  10.6 13.9 %copy-start.8 = (bf16[84,512]{1,0:T(8,128)(2,1)S(1)}, bf16[84,512]{1,0:T(8,128)(2,1)}, u32[]{:S(2)}) copy-start(bf16[84,512]{1,0:T(8,128)(2,1)} %param.28) | copy-start | bytes 258052
  27.4 12.4 %copy-start.10 = (s32[256,32]{0,1:T(8,128)S(1)}, s32[256,32]{0,1:T(8,128)}, u32[]{:S(2)}) copy-start(s32[256,32]{0,1:T(8,128)} %param.27) | copy-start | bytes 98308
  27.4 12.5 %copy-start.9 = (s32[4096]{0:T(1024)S(1)}, s32[4096]{0:T(1024)}, u32[]{:S(2)}) copy-start(s32[4096]{0:T(1024)} %param.23) | copy-start | bytes 49156
  27.4 105.3 %all-to-all-start = ((bf16[32,128,512]{2,1,0:T(8,128)(2,1)}), bf16[32,128,512]{2,1,0:T(8,128)(2,1)}, u32[]{:S(2)}, u32[]{:S(2)}) async-start(bf16[32,128,512]{2,1,0:T(8,128)(2,1)} %bitcast.94), calls=%async_computation | async-start | bytes 8388608 | tf_op jit(solution)/shard_map/all_to_all | solution.py:99
  39.7 471.3 %all-reduce.2.cloned.1.call-start = ((), (), s32[]{:S(2)}) async-start(), calls=%async_computation.1 | async-start | bytes 2097152 | tf_op jit(solution)/shard_map/psum | solution.py:144
  132.7 20.1 %copy-start.16 = (bf16[4,4096]{1,0:T(4,128)(2,1)S(1)}, bf16[4,4096]{1,0:T(4,128)(2,1)}, u32[]{:S(2)}) copy-start(bf16[4,4096]{1,0:T(4,128)(2,1)} %param.25) | copy-start | bytes 98308
  132.7 20.1 %copy-start.17 = (s32[4096]{0:T(1024)S(1)}, s32[4096]{0:T(1024)}, u32[]{:S(2)}) copy-start(s32[4096]{0:T(1024)} %param.24) | copy-start | bytes 49156
  132.7 20.1 %copy-start.18 = (bf16[4,512]{1,0:T(4,128)(2,1)S(1)}, bf16[4,512]{1,0:T(4,128)(2,1)}, u32[]{:S(2)}) copy-start(bf16[4,512]{1,0:T(4,128)(2,1)} %param.29) | copy-start | bytes 12292
  152.8 6.4 %copy-start.6 = (bf16[512,512]{1,0:T(8,128)(2,1)S(1)}, bf16[512,512]{1,0:T(8,128)(2,1)}, u32[]{:S(2)}) copy-start(bf16[512,512]{1,0:T(8,128)(2,1)} %param.30) | copy-start | bytes 1572868
  152.9 7.1 %copy-start.4 = (bf16[256,512]{1,0:T(8,128)(2,1)S(1)}, bf16[256,512]{1,0:T(8,128)(2,1)}, u32[]{:S(2)}) copy-start(bf16[256,512]{1,0:T(8,128)(2,1)} %param.26) | copy-start | bytes 786436
  152.9 7.1 %copy-start.11 = (f32[512]{0:T(512)S(1)}, f32[512]{0:T(512)}, u32[]{:S(2)}) copy-start(f32[512]{0:T(512)} %param.31) | copy-start | bytes 6148
  152.9 7.9 %copy-start.15 = (f32[512]{0:T(512)S(1)}, f32[512]{0:T(512)}, u32[]{:S(2)}) copy-start(f32[512]{0:T(512)} %param.32) | copy-start | bytes 6148
  159.9 0.8 copy-start.1
  159.9 1.5 copy-start.13
  168.8 0.7 copy-start.5
  169.5 8.7 %collective-permute-start = (bf16[128,1024]{1,0:T(8,128)(2,1)S(1)}, bf16[128,1024]{1,0:T(8,128)(2,1)S(1)}, u32[]{:S(2)}, u32[]{:S(2)}) collective-permute-start(bf16[128,1024]{1,0:T(8,128)(2,1)S(1)} %get-tuple-element.45), channel_id=1, source_target_pairs={{0,1},{1,2},{2,3},{3,4},{4,5},{5,6},{6,7},{7,8},{8,9},{9,10},{10,1... | collective-permute-start | bytes 786440 | tf_op jit(solution)/shard_map/ppermute | solution.py:27
  172.1 7.0 %collective-permute-start.1 = (bf16[128,1024]{1,0:T(8,128)(2,1)S(1)}, bf16[128,1024]{1,0:T(8,128)(2,1)}, u32[]{:S(2)}, u32[]{:S(2)}) collective-permute-start(bf16[128,1024]{1,0:T(8,128)(2,1)S(1)} %get-tuple-element.46), channel_id=1, source_target_pairs={{1,0},{2,1},{3,2},{4,3},{5,4},{6,5},{7,6},{8,7},{9,8},{10,9},{11,1... | collective-permute-start | bytes 786440 | tf_op jit(solution)/shard_map/ppermute | solution.py:28
  178.3 0.7 copy-start.7
  180.4 74.3 %copy-start.2 = (f32[256,512]{1,0:T(8,128)S(1)}, f32[256,512]{1,0:T(8,128)}, u32[]{:S(2)}) copy-start(f32[256,512]{1,0:T(8,128)} %copy-done.1) | copy-start | bytes 1572868
  180.4 74.3 %copy-start.12 = (f32[512]{0:T(512)S(1)}, f32[512]{0:T(512)}, u32[]{:S(2)}) copy-start(f32[512]{0:T(512)} %param.31) | copy-start | bytes 6148
  180.4 74.3 %copy-start.14 = (f32[256]{0:T(256)S(1)}, f32[256]{0:T(256)}, u32[]{:S(2)}) copy-start(f32[256]{0:T(256)} %copy-done.13) | copy-start | bytes 3076
  203.3 3.4 copy-start.3
  239.3 3.4 copy-start.3
Sparse Core Ops, SparseCore 0:
  254.8 256.0 all-reduce.1
where the time goes:
time: 522 us; the launch traced here: 520 us
  waiting for transfers between devices  347 us (66%)
  local copies, waits for them, and re-layouts  92.3 us (18%)
  matrix products  26.3 us (5%)
  other arithmetic  21.8 us (4%)
  starting transfers between devices  17.2 us (3%)
  between operations  15.2 us (3%)
    psum x1, waiting for transfers between devices, body(): out_grad = lax.psum(partial_value, ('noise', 'region'))  254 us
    all_to_all x1, waiting for transfers between devices, body(): lax.all_to_all(embedded.reshape(regions, slots, width), 'region', split_a...  92.8 us
    gather x2, local copies, waits for them, and re-layouts, attend(): nearby = jnp.take(padded, index_block, axis=0)  36.5 us
    gather x1, local copies, waits for them, and re-layouts, body(): source_rows = jnp.take(row_table, edge_src, axis=0)  20.1 us
    all_to_all x1, starting transfers between devices, body(): lax.all_to_all(embedded.reshape(regions, slots, width), 'region', split_a...  12.3 us
    gather x1, local copies, waits for them, and re-layouts, body(): picked = jnp.take(grid_in, send_list, axis=1)  12.1 us
  transfers between devices with their start and end apart: 4, of which 3 were waited for; matrix products, arithmetic and copies ran while one was open for 1% of the time, Pallas kernels for 0%

commit v1 on v0

v1 whole, which is shorter than its diff:
```python
import math

import jax
import jax.numpy as jnp
from jax import lax
from jax.experimental import pallas as pl
from jax.experimental.pallas import tpu as pltpu
from jax.sharding import PartitionSpec as P

BF = jnp.bfloat16
F32 = jnp.float32

D = 512
HEADS = 4
HEAD = 128
VARS = 84
VPAD = 96
GEO = 4
PLAN = 20
K_NB = 32
HALO = 128
NODES = 256
GRID = 2048
EDGES = 4096
SLOT = 128
REGIONS = 32
PLANES = 8
ROWS = 4
XS = 4
ETILE = 512
HALF = GRID // 2
KCAT = 128

sigma_max = 80.0
sigma_min = 0.03
plan_rho = 7.0
norm_eps = 1e-05
head_eps = 1e-06

UP_ROOT = sigma_max ** (1.0 / plan_rho)
LOW_ROOT = sigma_min ** (1.0 / plan_rho)

NT = (((1,), (1,)), ((), ()))


def dot(a, b):
    return jnp.dot(a, b, preferred_element_type=F32)


def dot_nt(a, b):
    return lax.dot_general(a, b, NT, preferred_element_type=F32)


def one_hot(code_row, rows):
    n = code_row.shape[1]
    ids = lax.broadcasted_iota(jnp.int32, (rows, n), 0).astype(F32).astype(BF)
    want = jnp.broadcast_to(code_row, (rows, n))
    return jnp.where(ids == want, jnp.ones((), BF), jnp.zeros((), BF))


def lanes(ref, first, count):
    return jnp.concatenate([ref[pl.ds(first + k, 1), :] for k in range(count)], axis=1)


def rms(values, epsilon):
    return values * lax.rsqrt(jnp.mean(values * values, axis=-1, keepdims=True) + epsilon)


def units(projected):
    return [
        rms(projected[:, h * HEAD : (h + 1) * HEAD], head_eps).astype(BF) for h in range(HEADS)
    ]


def with_ones(values):
    return jnp.concatenate([values, jnp.ones(values.shape, BF)], axis=1)


def plane_offset(i):
    half = lax.div(i + 1, 2)
    return lax.rem(4 + half * (1 - 2 * lax.rem(i, 2)) + PLANES, PLANES)


def kernel(
    level_ref,
    send_hbm,
    esrc_hbm,
    edst_hbm,
    nb_hbm,
    target_hbm,
    noise_hbm,
    geom_hbm,
    mesh_hbm,
    gw_hbm,
    ew_hbm,
    mw_hbm,
    eg_hbm,
    ag_hbm,
    qkv_hbm,
    ow_hbm,
    cot_hbm,
    mesh_out_ref,
    grad_ref,
    send_v,
    esrc_v,
    edst_v,
    nb_v,
    target_v,
    noise_v,
    geom_v,
    mesh_v,
    gw_v,
    ew_v,
    mw_v,
    eg_v,
    ag_v,
    qkv_v,
    ow_v,
    cot_v,
    in_sem,
    g_v,
    sbuf,
    rbuf,
    code_v,
    jbit_v,
    dstf_v,
    wc_v,
    wt_v,
    acc_v,
    node_v,
    hid_v,
    count_l,
    count_h,
    enc_v,
    nrm_v,
    halo_v,
    att_v,
    attt_v,
    a2a_send,
    a2a_recv,
    halo_send,
    halo_recv,
    p_v,
    sb1,
    rb1,
    sb2,
    rb2,
    own3,
    sb3,
    rb3,
    fbuf,
    s1_send,
    s1_recv,
    s2_send,
    s2_recv,
    s3_send,
    s3_recv,
    g3_send,
    g3_recv,
    g2_send,
    g2_recv,
    g1_send,
    g1_recv,
):
    noise = lax.axis_index("noise")
    me = lax.axis_index("region")
    core = lax.rem(noise, 2)
    mx = lax.div(noise, 2)
    mz = lax.div(me, ROWS)
    partner = noise + 1 - 2 * core
    region_next = lax.rem(me + 1, REGIONS)
    region_prev = lax.rem(me + REGIONS - 1, REGIONS)

    def x_peer(d):
        return lax.rem(mx + d, XS) * 2 + core

    pairs = [
        (noise_hbm.at[0], noise_v),
        (target_hbm, target_v),
        (send_hbm.at[0], send_v),
        (esrc_hbm, esrc_v),
        (edst_hbm, edst_v),
        (nb_hbm, nb_v),
        (geom_hbm, geom_v),
        (gw_hbm, gw_v),
        (ew_hbm, ew_v),
        (mw_hbm, mw_v),
        (mesh_hbm, mesh_v),
        (eg_hbm, eg_v),
        (ag_hbm, ag_v),
        (qkv_hbm, qkv_v),
        (cot_hbm.at[0], cot_v),
        (ow_hbm, ow_v),
    ]
    loads = [pltpu.make_async_copy(s, d, in_sem.at[i]) for i, (s, d) in enumerate(pairs)]
    (
        ld_noise,
        ld_target,
        ld_send,
        ld_esrc,
        ld_edst,
        ld_nb,
        ld_geom,
        ld_gw,
        ld_ew,
        ld_mw,
        ld_mesh,
        ld_eg,
        ld_ag,
        ld_qkv,
        ld_cot,
        ld_ow,
    ) = loads
    for load in loads:
        load.start()

    barrier = pltpu.get_barrier_semaphore()

    def tell(i, carry):
        pl.semaphore_signal(
            barrier,
            inc=1,
            device_id={"region": lax.rem(me + i, REGIONS)},
            device_id_type=pl.DeviceIdType.MESH,
        )
        return carry

    lax.fori_loop(1, REGIONS, tell, 0)
    for d in range(1, XS):
        pl.semaphore_signal(
            barrier, inc=1, device_id={"noise": x_peer(d)}, device_id_type=pl.DeviceIdType.MESH
        )
    pl.semaphore_signal(
        barrier, inc=1, device_id={"noise": partner}, device_id_type=pl.DeviceIdType.MESH
    )

    g_v[80:96, :] = jnp.zeros((16, HALF), BF)
    g_v[176:192, :] = jnp.zeros((16, HALF), BF)
    level = level_ref[0].astype(F32) * (1.0 / (PLAN - 1))
    root = UP_ROOT + level * (LOW_ROOT - UP_ROOT)
    root2 = root * root
    sigma = root2 * root2 * root2 * root
    ld_noise.wait()
    ld_target.wait()
    scale = lax.rsqrt(jnp.full((1, HALF), 1.0 + sigma * sigma, F32))
    for part in range(2):
        cols = slice(part * HALF, (part + 1) * HALF)
        noised = (
            target_v[:, cols].astype(F32) + sigma * noise_v[:, cols].astype(F32)
        ) * scale
        g_v[part * VPAD : part * VPAD + VARS, :] = noised.astype(BF)
    ld_send.wait()
    pl.semaphore_wait(barrier, REGIONS - 1 + XS - 1 + 1)

    def send_plane(i, carry):
        z = lax.rem(mz + plane_offset(i), PLANES)
        idx = lanes(send_v, ROWS * z, ROWS)
        upper = idx >= HALF
        low = jnp.where(upper, idx - HALF, idx).astype(F32)
        hot = jnp.concatenate(
            [one_hot((low - 256.0 * k).astype(BF), 256) for k in range(HALF // 256)], axis=0
        )
        both = dot(g_v[...], hot)
        picked = jnp.where(upper, both[VPAD:, :], both[:VPAD, :]).astype(BF)
        for k in range(ROWS):
            r = ROWS * z + k
            sbuf[r] = picked[:, k * SLOT : (k + 1) * SLOT]

            @pl.when(r != me)
            def _():
                pltpu.make_async_remote_copy(
                    src_ref=sbuf.at[r],
                    dst_ref=rbuf.at[me],
                    send_sem=a2a_send,
                    recv_sem=a2a_recv.at[mz],
                    device_id={"region": r},
                    device_id_type=pl.DeviceIdType.MESH,
                ).start()

            @pl.when(r == me)
            def _():
                pltpu.make_async_copy(sbuf.at[r], rbuf.at[me], a2a_recv.at[mz]).start()

        return carry

    with jax.named_scope("send_columns"):
        lax.fori_loop(0, PLANES, send_plane, 0)

    with jax.named_scope("tables"):
        ld_esrc.wait()
        ld_edst.wait()
        src = esrc_v[...]
        code_v[...] = (
            (src >> 9) * 256 + ((src >> 8) & 1) * 128 + (src & 127)
        ).astype(F32)
        jbit_v[...] = (src >> 7) & 1
        dstf_v[...] = edst_v[...].astype(F32)
        acc_v[...] = jnp.zeros((KCAT, EDGES), BF)
        ld_geom.wait()
        acc_v[VPAD : VPAD + GEO, :] = geom_v[...]
        ld_gw.wait()
        ld_ew.wait()
        wc_v[...] = jnp.zeros((KCAT, D), F32)
        wc_v[0:VARS, :] = gw_v[...].astype(F32)
        wc_v[VPAD : VPAD + GEO, :] = ew_v[...].astype(F32)
        wt_v[...] = wc_v[...].T.astype(BF)
        for e in range(EDGES // ETILE):
            row = lanes(dstf_v, e * (ETILE // 128), ETILE // 128).astype(BF)
            node_v[:, e * ETILE : (e + 1) * ETILE] = one_hot(row, NODES)
        ld_nb.wait()
        local = nb_v[...] - me * NODES + HALO
        local = jnp.where(local < 0, local + NODES * REGIONS, local)
        local = jnp.where(local >= NODES * REGIONS, local - NODES * REGIONS, local)
        for block in range(NODES // 32):
            rows = slice(block * 32, (block + 1) * 32)
            ids = lax.broadcasted_iota(jnp.int32, (32, NODES), 1)
            ids_l = ids + HALO
            ids_h = jnp.where(ids < HALO, ids, ids + NODES)
            total_l = jnp.zeros((32, NODES), F32)
            total_h = jnp.zeros((32, NODES), F32)
            for j in range(K_NB):
                at = local[rows, j : j + 1]
                total_l = total_l + jnp.where(ids_l == at, 1.0, 0.0)
                total_h = total_h + jnp.where(ids_h == at, 1.0, 0.0)
            count_l[rows, :] = total_l
            count_h[rows, :] = total_h

    def gather_plane(i, carry):
        z = lax.rem(mz + PLANES - plane_offset(i), PLANES)
        window = rbuf.at[pl.ds(ROWS * z, ROWS)]
        pltpu.make_async_copy(window, window, a2a_recv.at[z]).wait()
        table = jnp.concatenate(
            [
                jnp.concatenate([rbuf[ROWS * z], rbuf[ROWS * z + 1]], axis=0),
                jnp.concatenate([rbuf[ROWS * z + 2], rbuf[ROWS * z + 3]], axis=0),
            ],
            axis=1,
        )
        base = (z * 256).astype(F32)
        for e in range(EDGES // ETILE):
            first = e * (ETILE // 128)
            cols = slice(e * ETILE, (e + 1) * ETILE)
            hot = one_hot((lanes(code_v, first, ETILE // 128) - base).astype(BF), 256)
            both = dot(table, hot)
            odd = lanes(jbit_v, first, ETILE // 128) == 1
            picked = jnp.where(odd, both[VPAD:, :], both[:VPAD, :]).astype(BF)
            acc_v[0:VPAD, cols] = acc_v[0:VPAD, cols] + picked
        return carry

    with jax.named_scope("gather_edges"):
        lax.fori_loop(0, PLANES, gather_plane, 0)

    with jax.named_scope("hidden"):
        for e in range(EDGES // ETILE):
            cols = slice(e * ETILE, (e + 1) * ETILE)
            x = dot(wt_v[...], acc_v[:, cols])
            half = 0.5 * x
            hid_v[:, cols] = (half + half * jnp.tanh(half)).astype(BF)
        hidden_sum = dot_nt(node_v[...], hid_v[...])

    with jax.named_scope("encode"):
        ld_mw.wait()
        ld_mesh.wait()
        ld_eg.wait()
        ld_ag.wait()
        high = hidden_sum.astype(BF)
        rest = (hidden_sum - high.astype(F32)).astype(BF)
        aggregate = dot(high, mw_v[...]) + dot(rest, mw_v[...])
        encoded = mesh_v[...].astype(F32) + rms(aggregate, norm_eps) * eg_v[...]
        enc_v[...] = encoded
        nrm_v[...] = (rms(encoded, norm_eps) * ag_v[...]).astype(BF)

    to_prev = pltpu.make_async_remote_copy(
        src_ref=nrm_v.at[0:HALO],
        dst_ref=halo_v.at[HALO : 2 * HALO],
        send_sem=halo_send.at[0],
        recv_sem=halo_recv.at[0],
        device_id={"region": region_prev},
        device_id_type=pl.DeviceIdType.MESH,
    )
    to_next = pltpu.make_async_remote_copy(
        src_ref=nrm_v.at[NODES - HALO : NODES],
        dst_ref=halo_v.at[0:HALO],
        send_sem=halo_send.at[1],
        recv_sem=halo_recv.at[1],
        device_id={"region": region_next},
        device_id_type=pl.DeviceIdType.MESH,
    )
    to_prev.start()
    to_next.start()

    with jax.named_scope("attention_local"):
        ld_qkv.wait()
        projected = dot(nrm_v[...], qkv_v[...])
        query = units(projected[:, :D])
        key = units(projected[:, D : 2 * D])
        value = projected[:, 2 * D :].astype(BF)
        rate = 1.0 / math.sqrt(HEAD)

        def mix(q, k, v, count):
            weight = (jnp.exp(dot_nt(q, k) * rate) * count).astype(BF)
            return dot(weight, with_ones(v))

        mixed = [
            mix(query[h], key[h], value[:, h * HEAD : (h + 1) * HEAD], count_l[...])
            for h in range(HEADS)
        ]

    with jax.named_scope("attention_halo"):
        to_prev.wait()
        to_next.wait()
        beside = dot(halo_v[...], qkv_v[:, D:])
        key = units(beside[:, :D])
        value = beside[:, D:].astype(BF)
        for h in range(HEADS):
            both = mixed[h] + mix(
                query[h], key[h], value[:, h * HEAD : (h + 1) * HEAD], count_h[...]
            )
            att_v[:, h * HEAD : (h + 1) * HEAD] = both[:, :HEAD] / both[:, HEAD:]
        attt_v[...] = att_v[...].T.astype(BF)

    def quarter(i):
        return lax.rem(mx + (2, 1, 3, 0)[i], XS)

    with jax.named_scope("gradient_term"):
        ld_cot.wait()
        other = pl.multiple_of((1 - core) * NODES, NODES)
        mine = pl.multiple_of(core * NODES, NODES)
        sb1[...] = dot(attt_v[pl.ds(other, NODES), :], cot_v[...]).astype(BF)
        firsts = []
        for i in range(XS):
            rows = pl.ds(pl.multiple_of(quarter(i) * 64, 64), 64)
            copy = pltpu.make_async_remote_copy(
                src_ref=sb1.at[rows],
                dst_ref=rb1.at[rows],
                send_sem=s1_send.at[i],
                recv_sem=s1_recv.at[i],
                device_id={"noise": partner},
                device_id_type=pl.DeviceIdType.MESH,
            )
            copy.start()
            firsts.append(copy)
        p_v[...] = dot(attt_v[pl.ds(mine, NODES), :], cot_v[...])

    with jax.named_scope("reduce_x"):
        seconds = []
        for i in range(XS):
            rows = pl.ds(pl.multiple_of(quarter(i) * 64, 64), 64)
            firsts[i].wait_recv()
            total = p_v[rows, :] + rb1[rows, :].astype(F32)
            if i < XS - 1:
                d = (2, 1, 3)[i]
                sb2[i] = total.astype(BF)
                copy = pltpu.make_async_remote_copy(
                    src_ref=sb2.at[i],
                    dst_ref=rb2.at[i],
                    send_sem=s2_send.at[i],
                    recv_sem=s2_recv.at[i],
                    device_id={"noise": x_peer(d)},
                    device_id_type=pl.DeviceIdType.MESH,
                )
                copy.start()
                seconds.append(copy)
            else:
                own3[...] = total

    with jax.named_scope("mesh_out"):
        ld_ow.wait()
        mesh_out_ref[...] = (
            enc_v[...] + dot(att_v[...].astype(BF), ow_v[...])
        ).astype(BF)

    tile_me = lax.div(me, 2)
    owner = lax.rem(me, 2) == core

    def tile_of(t):
        return (
            pl.ds(pl.multiple_of(lax.div(t, 4) * 16, 16), 16),
            pl.ds(pl.multiple_of(lax.rem(t, 4) * 128, 128), 128),
        )

    with jax.named_scope("reduce_region"):
        for copy in seconds:
            copy.wait_recv()
        total = own3[...]
        for i in range(XS - 1):
            total = total + rb2[i].astype(F32)
        own3[...] = total
        sb3[...] = total.astype(BF)

        def send_tile(i, carry):
            t = lax.rem(tile_me + i, 16)
            to = 2 * t + core
            rows, cols = tile_of(t)

            @pl.when(to != me)
            def _():
                pltpu.make_async_remote_copy(
                    src_ref=sb3.at[rows, cols],
                    dst_ref=rb3.at[lax.rem(me - to + REGIONS, REGIONS) - 1],
                    send_sem=s3_send,
                    recv_sem=s3_recv,
                    device_id={"region": to},
                    device_id_type=pl.DeviceIdType.MESH,
                ).start()

            return carry

        lax.fori_loop(0, 16, send_tile, 0)

    quarter_row = pl.multiple_of(core * NODES + mx * 64, 64)
    own_rows = pl.ds(pl.multiple_of(quarter_row + lax.div(tile_me, 4) * 16, 16), 16)
    own_cols = pl.ds(pl.multiple_of(lax.rem(tile_me, 4) * 128, 128), 128)

    with jax.named_scope("gather_region"):

        @pl.when(owner)
        def _():
            pltpu.make_async_copy(rb3, rb3, s3_recv).wait()
            rows, cols = tile_of(tile_me)
            total = own3[rows, cols]
            for i in range(REGIONS - 1):
                total = total + rb3[i].astype(F32)
            fbuf[own_rows, own_cols] = total.astype(BF)

            def send_own(i, carry):
                pltpu.make_async_remote_copy(
                    src_ref=fbuf.at[own_rows, own_cols],
                    dst_ref=fbuf.at[own_rows, own_cols],
                    send_sem=g3_send,
                    recv_sem=g3_recv,
                    device_id={"region": lax.rem(me + i, REGIONS)},
                    device_id_type=pl.DeviceIdType.MESH,
                ).start()
                return carry

            lax.fori_loop(1, REGIONS, send_own, 0)
            got = rb3.at[0:15]
            pltpu.make_async_copy(got, got, g3_recv).wait()

        @pl.when(jnp.logical_not(owner))
        def _():
            got = rb3.at[0:16]
            pltpu.make_async_copy(got, got, g3_recv).wait()

    with jax.named_scope("gather_x"):
        mine4 = pl.ds(quarter_row, 64)
        thirds = []
        for i, d in enumerate((2, 1, 3)):
            copy = pltpu.make_async_remote_copy(
                src_ref=fbuf.at[mine4],
                dst_ref=fbuf.at[mine4],
                send_sem=g2_send.at[i],
                recv_sem=g2_recv.at[i],
                device_id={"noise": x_peer(d)},
                device_id_type=pl.DeviceIdType.MESH,
            )
            copy.start()
            thirds.append(copy)
        lasts = []
        for i, d in enumerate((0, 1, 3, 2)):
            rows = pl.ds(pl.multiple_of(core * NODES + lax.rem(mx + XS - d, XS) * 64, 64), 64)
            if d:
                thirds[(2, 1, 3).index(d)].wait_recv()
            copy = pltpu.make_async_remote_copy(
                src_ref=fbuf.at[rows],
                dst_ref=fbuf.at[rows],
                send_sem=g1_send.at[i],
                recv_sem=g1_recv.at[i],
                device_id={"noise": partner},
                device_id_type=pl.DeviceIdType.MESH,
            )
            copy.start()
            lasts.append(copy)
        for copy in lasts:
            copy.wait_recv()
        grad_ref[...] = fbuf[...]

    sent = sbuf.at[0 : REGIONS - 1]
    pltpu.make_async_copy(sent, sent, a2a_send).wait()
    for copy in firsts + seconds + thirds + lasts:
        copy.wait_send()

    @pl.when(owner)
    def _():
        pltpu.make_async_copy(rb3, rb3, g3_send).wait()
        some = rb3.at[0:15]
        pltpu.make_async_copy(some, some, s3_send).wait()

    @pl.when(jnp.logical_not(owner))
    def _():
        some = rb3.at[0:16]
        pltpu.make_async_copy(some, some, s3_send).wait()


def body(
    target_state,
    noise_field,
    level_index,
    send_rows,
    edge_src,
    edge_dst,
    edge_geom,
    mesh_init,
    neighbours,
    grid_weight,
    edge_weight,
    message_weight,
    enc_gain,
    att_gain,
    qkv_weight,
    out_weight,
    cotangent,
):
    operands = (
        level_index,
        send_rows,
        edge_src.reshape(EDGES // 128, 128),
        edge_dst.reshape(EDGES // 128, 128),
        neighbours,
        target_state,
        noise_field,
        edge_geom,
        mesh_init,
        grid_weight,
        edge_weight,
        message_weight,
        enc_gain.reshape(1, D),
        att_gain.reshape(1, D),
        qkv_weight,
        out_weight,
        cotangent,
    )
    vmem = pltpu.VMEM
    dma = pltpu.SemaphoreType.DMA
    i32 = jnp.int32
    scratch = [
        vmem((REGIONS, SLOT), i32),
        vmem((EDGES // 128, 128), i32),
        vmem((EDGES // 128, 128), i32),
        vmem((NODES, K_NB), i32),
        vmem((VARS, GRID), BF),
        vmem((VARS, GRID), BF),
        vmem((GEO, EDGES), BF),
        vmem((NODES, D), BF),
        vmem((VARS, D), BF),
        vmem((GEO, D), BF),
        vmem((D, D), BF),
        vmem((1, D), F32),
        vmem((1, D), F32),
        vmem((D, 3 * D), BF),
        vmem((D, D), BF),
        vmem((NODES, D), BF),
        dma((16,)),
        vmem((2 * VPAD, HALF), BF),
        vmem((REGIONS, VPAD, SLOT), BF),
        vmem((REGIONS, VPAD, SLOT), BF),
        vmem((EDGES // 128, 128), F32),
        vmem((EDGES // 128, 128), i32),
        vmem((EDGES // 128, 128), F32),
        vmem((KCAT, D), F32),
        vmem((D, KCAT), BF),
        vmem((KCAT, EDGES), BF),
        vmem((NODES, EDGES), BF),
        vmem((D, EDGES), BF),
        vmem((NODES, NODES), F32),
        vmem((NODES, NODES), F32),
        vmem((NODES, D), F32),
        vmem((NODES, D), BF),
        vmem((2 * HALO, D), BF),
        vmem((NODES, D), F32),
        vmem((D, NODES), BF),
        dma,
        dma((PLANES,)),
        dma((2,)),
        dma((2,)),
        vmem((NODES, D), F32),
        vmem((NODES, D), BF),
        vmem((NODES, D), BF),
        vmem((XS - 1, 64, D), BF),
        vmem((XS - 1, 64, D), BF),
        vmem((64, D), F32),
        vmem((64, D), BF),
        vmem((REGIONS - 1, 16, 128), BF),
        vmem((D, D), BF),
        dma((XS,)),
        dma((XS,)),
        dma((XS - 1,)),
        dma((XS - 1,)),
        dma,
        dma,
        dma,
        dma,
        dma((XS - 1,)),
        dma((XS - 1,)),
        dma((XS,)),
        dma((XS,)),
    ]
    mesh_out, grad = pl.pallas_call(
        kernel,
        out_shape=(
            jax.ShapeDtypeStruct((NODES, D), BF),
            jax.ShapeDtypeStruct((D, D), BF),
        ),
        in_specs=[pl.BlockSpec(memory_space=pltpu.SMEM)]
        + [pl.BlockSpec(memory_space=pl.ANY)] * (len(operands) - 1),
        out_specs=(
            pl.BlockSpec(memory_space=pltpu.VMEM),
            pl.BlockSpec(memory_space=pltpu.VMEM),
        ),
        scratch_shapes=scratch,
        compiler_params=pltpu.CompilerParams(
            collective_id=0, has_side_effects=True, vmem_limit_bytes=60 * 1024 * 1024
        ),
        cost_estimate=pl.CostEstimate(
            flops=12_000_000_000, bytes_accessed=6_000_000, transcendentals=3_000_000
        ),
    )(*operands)
    return mesh_out[None], grad.astype(F32)


def solution(mesh):
    in_specs = (
        P(None, "region"),
        P("noise", None, "region"),
        P("noise"),
        P("region", None, None),
        P("region"),
        P("region"),
        P(None, "region"),
        P("region", None),
        P("region", None),
        P(),
        P(),
        P(),
        P(),
        P(),
        P(),
        P(),
        P("noise", "region", None),
    )
    out_specs = (P("noise", "region", None), P())
    return jax.shard_map(body, mesh=mesh, in_specs=in_specs, out_specs=out_specs, check_vma=False)
```

time: 522 us -> 76.8 us (0.15)
  waiting for transfers between devices: 347 us -> 0 us
  local copies, waits for them, and re-layouts: 92.3 us -> 2.22 us
  Pallas kernels: 0 us -> 70.9 us
  matrix products: 26.3 us -> 0 us
  other arithmetic: 21.8 us -> 2.19 us
  starting transfers between devices: 17.2 us -> 0 us
  between operations: 15.2 us -> 1.29 us
    psum x1 -> x0, waiting for transfers between devices: 254 us -> none  [body(): out_grad = lax.psum(partial_value, ('noise', 'region'))]
    all_to_all x1 -> x0, waiting for transfers between devices: 92.8 us -> none  [body(): lax.all_to_all(embedded.reshape(regions, slots, width), 'region', split_a...]
    pallas_call x0 -> x1, Pallas kernels: none -> 70.9 us  [body(): pl.pallas_call(kernel, out_shape=(jax.ShapeDtypeStruct((NODES, D), BF), j...]
    gather x4 -> x0, local copies, waits for them, and re-layouts: 68.7 us -> none  [the longest x2 36.5 us: attend(): nearby = jnp.take(padded, index_block, axis=0)]
    dot_general x10 -> x0, matrix products: 26.3 us -> none  [the longest x2 6.74 us: attend(): jnp.einsum('bhk,bkhd->bhd', weights, values_near, preferred_element_type=...]
    all_to_all x1 -> x0, starting transfers between devices: 12.3 us -> none  [body(): lax.all_to_all(embedded.reshape(regions, slots, width), 'region', split_a...]
    select_n x6 -> x0, other arithmetic: 9.81 us -> none  [the longest x4 9.06 us: attend(): nearby = jnp.take(padded, index_block, axis=0)]
    while x6 -> x0, local copies, waits for them, and re-layouts: 6.82 us -> none
  transfers between devices with their start and end apart: 4 -> 0, of which waited for: 3 -> 0; matrix products, arithmetic and copies ran while one was open for 1% -> 0% of each run, Pallas kernels for 0% -> 0%
where the time goes in v1:
time: 76.8 us; the launch traced here: 76.6 us
  Pallas kernels  70.9 us (92%)
  local copies, waits for them, and re-layouts  2.22 us (3%)
  other arithmetic  2.19 us (3%)
  between operations  1.29 us (2%)
    pallas_call x1, Pallas kernels, body(): pl.pallas_call(kernel, out_shape=(jax.ShapeDtypeStruct((NODES, D), BF), j...  70.9 us
    unnamed x4, local copies, waits for them, and re-layouts  2.22 us
    convert_element_type x1, other arithmetic, body(): return (mesh_out[None], grad.astype(F32))  2.19 us

profile of v1, /device:TPU:1, one launch (start us, length us, event | category | flops | bytes accessed | tf_op | source)
XLA Modules:
  0.0 76.6 jit_solution(14483664632734978064)
XLA Ops:
  1.3 1.5 %copy.19.nb_hbm = s32[256,32]{1,0:T(8,128)} copy(s32[256,32]{0,1:T(8,128)} %param.25) | data formatting | bytes 65536 | tf_op args[8]
  2.8 70.9 %shard_map.176 = (bf16[256,512]{1,0:T(8,128)(2,1)}, bf16[512,512]{1,0:T(8,128)(2,1)}) custom-call(s32[1]{0:T(128)S(6)} %copy.21.level_ref, s32[1,32,128]{2,1,0:T(8,128)} %send_hbm.1, s32[32,128]{1,0:T(8,128)} %bitcast.6, s32[32,128]{1,0:T(8,128)} %bitcast.7, s32[256,32]{1,0:T(8,128)} %copy.19.nb_hbm, bf16[84,2048]{1,0:T(8,128)(2,1)} %target_hbm.1, ...), custom_call_target="tpu_custom_call" | custom-call | flops 12000000000 | bytes 6000000 | tf_op jit(solution)/shard_map/pallas_call | solution.py:699
  73.7 0.0 copy-start
  73.7 2.2 %convert_element_type.3 = f32[512,512]{1,0:T(8,128)} convert(bf16[512,512]{1,0:T(8,128)(2,1)} %get-tuple-element.5) | non-fusion elementwise | flops 262144 | bytes 1572864 | tf_op jit(solution)/shard_map/convert_element_type | solution.py:719
  75.9 0.0 copy-done
  75.9 0.7 copy.22
Async XLA Ops:
  73.7 2.2 %copy-start = (bf16[256,512]{1,0:T(8,128)(2,1)S(1)}, bf16[256,512]{1,0:T(8,128)(2,1)}, u32[]{:S(2)}) copy-start(bf16[256,512]{1,0:T(8,128)(2,1)} %get-tuple-element.4) | copy-start | bytes 786436

commit v2 on v1

v2 whole, which is shorter than its diff:
```python
import math

import jax
import jax.numpy as jnp
from jax import lax
from jax.experimental import pallas as pl
from jax.experimental.pallas import tpu as pltpu
from jax.sharding import PartitionSpec as P

BF = jnp.bfloat16
F32 = jnp.float32

D = 512
HEADS = 4
HEAD = 128
VARS = 84
VPAD = 96
GEO = 4
PLAN = 20
K_NB = 32
HALO = 128
NODES = 256
GRID = 2048
EDGES = 4096
SLOT = 128
REGIONS = 32
PLANES = 8
ROWS = 4
XS = 4
ETILE = 512
HSPLIT = 8
HALF = GRID // 2
KCAT = 128

sigma_max = 80.0
sigma_min = 0.03
plan_rho = 7.0
norm_eps = 1e-05
head_eps = 1e-06

UP_ROOT = sigma_max ** (1.0 / plan_rho)
LOW_ROOT = sigma_min ** (1.0 / plan_rho)

AROUND = sorted(
    [(dx, dy) for dx in range(XS) for dy in range(ROWS) if dx or dy],
    key=lambda d: (-min(d[0], XS - d[0]) - min(d[1], ROWS - d[1]), d),
)

NT = (((1,), (1,)), ((), ()))


def dot(a, b):
    return jnp.dot(a, b, preferred_element_type=F32)


def dot_nt(a, b):
    return lax.dot_general(a, b, NT, preferred_element_type=F32)


def one_hot(code_row, rows):
    n = code_row.shape[1]
    ids = lax.broadcasted_iota(jnp.int32, (rows, n), 0).astype(F32).astype(BF)
    want = jnp.broadcast_to(code_row, (rows, n))
    return jnp.where(ids == want, jnp.ones((), BF), jnp.zeros((), BF))


def lanes(ref, first, count):
    return jnp.concatenate([ref[pl.ds(first + k, 1), :] for k in range(count)], axis=1)


def rms(values, epsilon):
    return values * lax.rsqrt(jnp.mean(values * values, axis=-1, keepdims=True) + epsilon)


def units(projected):
    return [
        rms(projected[:, h * HEAD : (h + 1) * HEAD], head_eps).astype(BF) for h in range(HEADS)
    ]


def with_ones(values):
    return jnp.concatenate([values, jnp.ones(values.shape, BF)], axis=1)


def plane_offset(i):
    half = lax.div(i + 1, 2)
    return lax.rem(4 + half * (1 - 2 * lax.rem(i, 2)) + PLANES, PLANES)


def kernel(
    level_ref,
    send_hbm,
    esrc_hbm,
    edst_hbm,
    nb_hbm,
    target_hbm,
    noise_hbm,
    geom_hbm,
    mesh_hbm,
    gw_hbm,
    ew_hbm,
    mw_hbm,
    eg_hbm,
    ag_hbm,
    qkv_hbm,
    ow_hbm,
    cot_hbm,
    mesh_out_ref,
    grad_ref,
    send_v,
    esrc_v,
    edst_v,
    nb_v,
    target_v,
    noise_v,
    geom_v,
    mesh_v,
    gw_v,
    ew_v,
    mw_v,
    eg_v,
    ag_v,
    qkv_v,
    ow_v,
    cot_v,
    in_sem,
    g_v,
    sbuf,
    rbuf,
    code_v,
    jbit_v,
    dstf_v,
    wc_v,
    wt_v,
    tab_v,
    acc_v,
    node_v,
    hid_v,
    count_t,
    count_l,
    count_h,
    enc_v,
    nrm_v,
    halo_v,
    att_v,
    attt_v,
    a2a_send,
    a2a_recv,
    halo_send,
    halo_recv,
    p_v,
    sb1,
    rb1,
    sb2,
    rb2,
    zbuf,
    fbuf,
    s1_send,
    s1_recv,
    s2_send,
    s2_recv,
    s3_send,
    s3_recv,
    g2_send,
    g2_recv,
    g1_send,
    g1_recv,
):
    noise = lax.axis_index("noise")
    me = lax.axis_index("region")
    core = lax.rem(noise, 2)
    mx = lax.div(noise, 2)
    mz = lax.div(me, ROWS)
    my = lax.rem(me, ROWS)
    partner = noise + 1 - 2 * core
    region_next = lax.rem(me + 1, REGIONS)
    region_prev = lax.rem(me + REGIONS - 1, REGIONS)

    def across(dx, dy):
        return {
            "noise": lax.rem(mx + dx, XS) * 2 + core,
            "region": mz * ROWS + lax.rem(my + dy, ROWS),
        }

    def piece(x, y):
        return pl.ds(pl.multiple_of((x * ROWS + y) * 16, 16), 16)

    pairs = [
        (noise_hbm.at[0], noise_v),
        (target_hbm, target_v),
        (send_hbm.at[0], send_v),
        (esrc_hbm, esrc_v),
        (edst_hbm, edst_v),
        (nb_hbm, nb_v),
        (geom_hbm, geom_v),
        (gw_hbm, gw_v),
        (ew_hbm, ew_v),
        (mw_hbm, mw_v),
        (mesh_hbm, mesh_v),
        (eg_hbm, eg_v),
        (ag_hbm, ag_v),
        (qkv_hbm, qkv_v),
        (cot_hbm.at[0], cot_v),
        (ow_hbm, ow_v),
    ]
    loads = [pltpu.make_async_copy(s, d, in_sem.at[i]) for i, (s, d) in enumerate(pairs)]
    (
        ld_noise,
        ld_target,
        ld_send,
        ld_esrc,
        ld_edst,
        ld_nb,
        ld_geom,
        ld_gw,
        ld_ew,
        ld_mw,
        ld_mesh,
        ld_eg,
        ld_ag,
        ld_qkv,
        ld_cot,
        ld_ow,
    ) = loads
    for load in loads[:3]:
        load.start()

    barrier = pltpu.get_barrier_semaphore()

    def tell(device):
        pl.semaphore_signal(
            barrier, inc=1, device_id=device, device_id_type=pl.DeviceIdType.MESH
        )

    def tell_region(i, carry):
        tell({"region": lax.rem(me + i, REGIONS)})
        return carry

    lax.fori_loop(1, REGIONS, tell_region, 0)
    beyond = [(dx, dy) for dx, dy in AROUND if dx]
    for dx, dy in beyond:
        tell(across(dx, dy))
    tell({"noise": partner})
    for load in loads[3:]:
        load.start()

    g_v[80:96, :] = jnp.zeros((16, HALF), BF)
    g_v[176:192, :] = jnp.zeros((16, HALF), BF)
    level = jnp.broadcast_to(level_ref[...], (1, HALF)).astype(F32) * (1.0 / (PLAN - 1))
    root = UP_ROOT + level * (LOW_ROOT - UP_ROOT)
    root2 = root * root
    sigma = root2 * root2 * root2 * root
    scale = lax.rsqrt(1.0 + sigma * sigma)
    ld_noise.wait()
    ld_target.wait()
    for part in range(2):
        cols = slice(part * HALF, (part + 1) * HALF)
        noised = (
            target_v[:, cols].astype(F32) + sigma * noise_v[:, cols].astype(F32)
        ) * scale
        g_v[part * VPAD : part * VPAD + VARS, :] = noised.astype(BF)
    ld_send.wait()
    pl.semaphore_wait(barrier, REGIONS - 1 + len(beyond) + 1)

    def send_plane(i, carry):
        z = lax.rem(mz + plane_offset(i), PLANES)
        idx = lanes(send_v, ROWS * z, ROWS)
        upper = idx >= HALF
        low = jnp.where(upper, idx - HALF, idx).astype(F32)
        hot = jnp.concatenate(
            [one_hot((low - 256.0 * k).astype(BF), 256) for k in range(HALF // 256)], axis=0
        )
        both = dot(g_v[...], hot)
        picked = jnp.where(upper, both[VPAD:, :], both[:VPAD, :]).astype(BF)
        for k in range(ROWS):
            r = ROWS * z + k
            sbuf[r] = picked[:VARS, k * SLOT : (k + 1) * SLOT]

            @pl.when(r != me)
            def _():
                pltpu.make_async_remote_copy(
                    src_ref=sbuf.at[r],
                    dst_ref=rbuf.at[me],
                    send_sem=a2a_send,
                    recv_sem=a2a_recv.at[mz],
                    device_id={"region": r},
                    device_id_type=pl.DeviceIdType.MESH,
                ).start()

            @pl.when(r == me)
            def _():
                pltpu.make_async_copy(sbuf.at[r], rbuf.at[me], a2a_recv.at[mz]).start()

        return carry

    with jax.named_scope("send_columns"):
        lax.fori_loop(0, PLANES, send_plane, 0)

    with jax.named_scope("tables"):
        ld_esrc.wait()
        ld_edst.wait()
        src = esrc_v[...]
        code_v[...] = (
            (src >> 9) * 256 + ((src >> 8) & 1) * 128 + (src & 127)
        ).astype(F32)
        jbit_v[...] = (src >> 7) & 1
        dstf_v[...] = edst_v[...].astype(F32)
        acc_v[...] = jnp.zeros((KCAT, EDGES), BF)
        tab_v[...] = jnp.zeros((2 * VPAD, 2 * SLOT), BF)
        ld_geom.wait()
        acc_v[VPAD : VPAD + GEO, :] = geom_v[...]
        ld_gw.wait()
        ld_ew.wait()
        wc_v[...] = jnp.zeros((KCAT, D), F32)
        wc_v[0:VARS, :] = gw_v[...].astype(F32)
        wc_v[VPAD : VPAD + GEO, :] = ew_v[...].astype(F32)
        wt_v[...] = wc_v[...].T.astype(BF)
        for e in range(EDGES // ETILE):
            row = lanes(dstf_v, e * (ETILE // 128), ETILE // 128).astype(BF)
            node_v[:, e * ETILE : (e + 1) * ETILE] = one_hot(row, NODES)
        ld_nb.wait()
        local = nb_v[...] - me * NODES + HALO
        local = jnp.where(local < 0, local + NODES * REGIONS, local)
        local = jnp.where(local >= NODES * REGIONS, local - NODES * REGIONS, local)
        for block in range(2 * NODES // 64):
            ids = lax.broadcasted_iota(jnp.int32, (64, NODES), 0) + block * 64
            total = jnp.zeros((64, NODES), F32)
            for j in range(K_NB):
                total = total + jnp.where(ids == local[j : j + 1, :], 1.0, 0.0)
            spot = slice(block * 64, (block + 1) * 64)
            count_t[spot, :] = total
        count_l[...] = count_t[HALO : HALO + NODES, :].T
        count_h[:, :HALO] = count_t[:HALO, :].T
        count_h[:, HALO:] = count_t[HALO + NODES :, :].T

    def gather_plane(i, carry):
        z = lax.rem(mz + PLANES - plane_offset(i), PLANES)
        window = rbuf.at[pl.ds(ROWS * z, ROWS)]
        pltpu.make_async_copy(window, window, a2a_recv.at[z]).wait()
        for k in range(ROWS):
            top, left = (k % 2) * VPAD, (k // 2) * SLOT
            tab_v[top : top + VARS, left : left + SLOT] = rbuf[ROWS * z + k]
        table = tab_v[...]
        base = (z * 256).astype(F32)
        for e in range(EDGES // ETILE):
            first = e * (ETILE // 128)
            cols = slice(e * ETILE, (e + 1) * ETILE)
            hot = one_hot((lanes(code_v, first, ETILE // 128) - base).astype(BF), 256)
            both = dot(table, hot)
            odd = lanes(jbit_v, first, ETILE // 128) == 1
            picked = jnp.where(odd, both[VPAD:, :], both[:VPAD, :]).astype(BF)
            acc_v[0:VPAD, cols] = acc_v[0:VPAD, cols] + picked
        return carry

    with jax.named_scope("gather_edges"):
        lax.fori_loop(0, PLANES, gather_plane, 0)

    with jax.named_scope("hidden"):
        for e in range(EDGES // ETILE):
            cols = slice(e * ETILE, (e + 1) * ETILE)
            x = dot(wt_v[...], acc_v[:, cols])
            half = 0.5 * x
            hid_v[:, cols] = (half + half * jnp.tanh(half)).astype(BF)
        hidden_sum = dot_nt(node_v[...], hid_v[...])

    with jax.named_scope("encode"):
        ld_mw.wait()
        ld_mesh.wait()
        ld_eg.wait()
        ld_ag.wait()
        high = hidden_sum.astype(BF)
        rest = (hidden_sum - high.astype(F32)).astype(BF)
        aggregate = dot(high, mw_v[...]) + dot(rest, mw_v[...])
        encoded = mesh_v[...].astype(F32) + rms(aggregate, norm_eps) * eg_v[...]
        enc_v[...] = encoded
        nrm_v[...] = (rms(encoded, norm_eps) * ag_v[...]).astype(BF)

    step = HALO // HSPLIT
    for part in range(HSPLIT):
        for side, first, there, to in (
            (0, 0, HALO, region_prev),
            (1, NODES - HALO, 0, region_next),
        ):
            pltpu.make_async_remote_copy(
                src_ref=nrm_v.at[first + part * step : first + (part + 1) * step],
                dst_ref=halo_v.at[there + part * step : there + (part + 1) * step],
                send_sem=halo_send,
                recv_sem=halo_recv,
                device_id={"region": to},
                device_id_type=pl.DeviceIdType.MESH,
            ).start()
    halo_sent = pltpu.make_async_copy(nrm_v, nrm_v, halo_send)
    halo_got = pltpu.make_async_copy(halo_v, halo_v, halo_recv)

    with jax.named_scope("attention_local"):
        ld_qkv.wait()
        projected = dot(nrm_v[...], qkv_v[...])
        query = units(projected[:, :D])
        key = units(projected[:, D : 2 * D])
        value = projected[:, 2 * D :].astype(BF)
        rate = 1.0 / math.sqrt(HEAD)

        def mix(q, k, v, count):
            weight = (jnp.exp(dot_nt(q, k) * rate) * count).astype(BF)
            return dot(weight, with_ones(v))

        mixed = [
            mix(query[h], key[h], value[:, h * HEAD : (h + 1) * HEAD], count_l[...])
            for h in range(HEADS)
        ]

    with jax.named_scope("attention_halo"):
        halo_got.wait()
        beside = dot(halo_v[...], qkv_v[:, D:])
        key = units(beside[:, :D])
        value = beside[:, D:].astype(BF)
        for h in range(HEADS):
            both = mixed[h] + mix(
                query[h], key[h], value[:, h * HEAD : (h + 1) * HEAD], count_h[...]
            )
            att_v[:, h * HEAD : (h + 1) * HEAD] = both[:, :HEAD] / both[:, HEAD:]
        attt_v[...] = att_v[...].T.astype(BF)

    with jax.named_scope("gradient_term"):
        ld_cot.wait()
        other = pl.multiple_of((1 - core) * NODES, NODES)
        mine = pl.multiple_of(core * NODES, NODES)
        sb1[...] = dot(attt_v[pl.ds(other, NODES), :], cot_v[...]).astype(BF)
        swap = pltpu.make_async_remote_copy(
            src_ref=sb1,
            dst_ref=rb1,
            send_sem=s1_send,
            recv_sem=s1_recv,
            device_id={"noise": partner},
            device_id_type=pl.DeviceIdType.MESH,
        )
        swap.start()
        p_v[...] = dot(attt_v[pl.ds(mine, NODES), :], cot_v[...])
        swap.wait_recv()

    with jax.named_scope("reduce_xy"):
        p_v[...] = p_v[...] + rb1[...].astype(F32)
        sb2[...] = p_v[...].astype(BF)
        for i, (dx, dy) in enumerate(AROUND):
            there = piece(lax.rem(mx + dx, XS), lax.rem(my + dy, ROWS))
            pltpu.make_async_remote_copy(
                src_ref=sb2.at[there],
                dst_ref=rb2.at[i],
                send_sem=s2_send,
                recv_sem=s2_recv,
                device_id=across(dx, dy),
                device_id_type=pl.DeviceIdType.MESH,
            ).start()

    with jax.named_scope("mesh_out"):
        ld_ow.wait()
        mesh_out_ref[...] = (
            enc_v[...] + dot(att_v[...].astype(BF), ow_v[...])
        ).astype(BF)

    with jax.named_scope("reduce_z"):
        pltpu.make_async_copy(rb2, rb2, s2_recv).wait()
        total = p_v[piece(mx, my), :]
        for i in range(len(AROUND)):
            total = total + rb2[i].astype(F32)
        zbuf[mz] = total.astype(BF)
        for d in (4, 3, 5, 2, 6, 1, 7):
            pltpu.make_async_remote_copy(
                src_ref=zbuf.at[mz],
                dst_ref=zbuf.at[mz],
                send_sem=s3_send,
                recv_sem=s3_recv,
                device_id={"region": lax.rem(me + ROWS * d, REGIONS)},
                device_id_type=pl.DeviceIdType.MESH,
            ).start()
        seven = zbuf.at[0 : PLANES - 1]
        pltpu.make_async_copy(seven, seven, s3_recv).wait()
        total = zbuf[0].astype(F32)
        for z in range(1, PLANES):
            total = total + zbuf[z].astype(F32)

    with jax.named_scope("gather_xy"):
        place = pl.ds(
            pl.multiple_of(core * NODES + (mx * ROWS + my) * 16, 16), 16
        )
        fbuf[place, :] = total.astype(BF)
        for dx, dy in AROUND:
            pltpu.make_async_remote_copy(
                src_ref=fbuf.at[place],
                dst_ref=fbuf.at[place],
                send_sem=g2_send,
                recv_sem=g2_recv,
                device_id=across(dx, dy),
                device_id_type=pl.DeviceIdType.MESH,
            ).start()
        pltpu.make_async_copy(rb2, rb2, g2_recv).wait()

    with jax.named_scope("gather_core"):
        half = pl.ds(mine, NODES)
        back = pltpu.make_async_remote_copy(
            src_ref=fbuf.at[half],
            dst_ref=fbuf.at[half],
            send_sem=g1_send,
            recv_sem=g1_recv,
            device_id={"noise": partner},
            device_id_type=pl.DeviceIdType.MESH,
        )
        back.start()
        back.wait_recv()
        grad_ref[...] = fbuf[...]

    sent = sbuf.at[0 : REGIONS - 1]
    pltpu.make_async_copy(sent, sent, a2a_send).wait()
    halo_sent.wait()
    swap.wait_send()
    pltpu.make_async_copy(rb2, rb2, s2_send).wait()
    pltpu.make_async_copy(seven, seven, s3_send).wait()
    pltpu.make_async_copy(rb2, rb2, g2_send).wait()
    back.wait_send()


def widen(mesh_hbm, grad_hbm, mesh_out_hbm, grad_out_hbm, narrow, wide, mesh_v, in_sems, out_sems):
    parts = [pl.ds(i * 128, 128) for i in range(4)]
    got = [
        pltpu.make_async_copy(grad_hbm.at[p], narrow.at[p], in_sems.at[i])
        for i, p in enumerate(parts)
    ]
    mesh_got = pltpu.make_async_copy(mesh_hbm, mesh_v, in_sems.at[4])
    for copy in got:
        copy.start()
    mesh_got.start()
    sent = []
    for i, p in enumerate(parts):
        got[i].wait()
        wide[p, :] = narrow[p, :].astype(F32)
        copy = pltpu.make_async_copy(wide.at[p], grad_out_hbm.at[p], out_sems.at[i])
        copy.start()
        sent.append(copy)
    mesh_got.wait()
    copy = pltpu.make_async_copy(mesh_v, mesh_out_hbm.at[0], out_sems.at[4])
    copy.start()
    for copy in sent + [copy]:
        copy.wait()


def body(
    target_state,
    noise_field,
    level_index,
    send_rows,
    edge_src,
    edge_dst,
    edge_geom,
    mesh_init,
    neighbours,
    grid_weight,
    edge_weight,
    message_weight,
    enc_gain,
    att_gain,
    qkv_weight,
    out_weight,
    cotangent,
):
    operands = (
        level_index.reshape(1, 1),
        send_rows,
        edge_src.reshape(EDGES // 128, 128),
        edge_dst.reshape(EDGES // 128, 128),
        neighbours.T,
        target_state,
        noise_field,
        edge_geom,
        mesh_init,
        grid_weight,
        edge_weight,
        message_weight,
        enc_gain.reshape(1, D),
        att_gain.reshape(1, D),
        qkv_weight,
        out_weight,
        cotangent,
    )
    vmem = pltpu.VMEM
    dma = pltpu.SemaphoreType.DMA
    i32 = jnp.int32
    scratch = [
        vmem((REGIONS, SLOT), i32),
        vmem((EDGES // 128, 128), i32),
        vmem((EDGES // 128, 128), i32),
        vmem((K_NB, NODES), i32),
        vmem((VARS, GRID), BF),
        vmem((VARS, GRID), BF),
        vmem((GEO, EDGES), BF),
        vmem((NODES, D), BF),
        vmem((VARS, D), BF),
        vmem((GEO, D), BF),
        vmem((D, D), BF),
        vmem((1, D), F32),
        vmem((1, D), F32),
        vmem((D, 3 * D), BF),
        vmem((D, D), BF),
        vmem((NODES, D), BF),
        dma((16,)),
        vmem((2 * VPAD, HALF), BF),
        vmem((REGIONS, VARS, SLOT), BF),
        vmem((REGIONS, VARS, SLOT), BF),
        vmem((EDGES // 128, 128), F32),
        vmem((EDGES // 128, 128), i32),
        vmem((EDGES // 128, 128), F32),
        vmem((KCAT, D), F32),
        vmem((D, KCAT), BF),
        vmem((2 * VPAD, 2 * SLOT), BF),
        vmem((KCAT, EDGES), BF),
        vmem((NODES, EDGES), BF),
        vmem((D, EDGES), BF),
        vmem((2 * NODES, NODES), F32),
        vmem((NODES, NODES), F32),
        vmem((NODES, NODES), F32),
        vmem((NODES, D), F32),
        vmem((NODES, D), BF),
        vmem((2 * HALO, D), BF),
        vmem((NODES, D), F32),
        vmem((D, NODES), BF),
        dma,
        dma((PLANES,)),
        dma,
        dma,
        vmem((NODES, D), F32),
        vmem((NODES, D), BF),
        vmem((NODES, D), BF),
        vmem((NODES, D), BF),
        vmem((len(AROUND), 16, D), BF),
        vmem((PLANES, 16, D), BF),
        vmem((D, D), BF),
    ] + [dma] * 10
    mesh_out, grad = pl.pallas_call(
        kernel,
        out_shape=(
            jax.ShapeDtypeStruct((NODES, D), BF),
            jax.ShapeDtypeStruct((D, D), BF),
        ),
        in_specs=[pl.BlockSpec(memory_space=pltpu.VMEM)]
        + [pl.BlockSpec(memory_space=pl.ANY)] * (len(operands) - 1),
        out_specs=(
            pl.BlockSpec(memory_space=pltpu.VMEM),
            pl.BlockSpec(memory_space=pltpu.VMEM),
        ),
        scratch_shapes=scratch,
        compiler_params=pltpu.CompilerParams(
            collective_id=0, has_side_effects=True, vmem_limit_bytes=60 * 1024 * 1024
        ),
        cost_estimate=pl.CostEstimate(
            flops=12_000_000_000, bytes_accessed=6_000_000, transcendentals=3_000_000
        ),
    )(*operands)
    mesh_out, grad = pl.pallas_call(
        widen,
        out_shape=(
            jax.ShapeDtypeStruct((1, NODES, D), BF),
            jax.ShapeDtypeStruct((D, D), F32),
        ),
        in_specs=[pl.BlockSpec(memory_space=pl.ANY)] * 2,
        out_specs=[pl.BlockSpec(memory_space=pl.ANY)] * 2,
        scratch_shapes=[
            vmem((D, D), BF),
            vmem((D, D), F32),
            vmem((NODES, D), BF),
            dma((5,)),
            dma((5,)),
        ],
    )(mesh_out, grad)
    return mesh_out, grad


def solution(mesh):
    in_specs = (
        P(None, "region"),
        P("noise", None, "region"),
        P("noise"),
        P("region", None, None),
        P("region"),
        P("region"),
        P(None, "region"),
        P("region", None),
        P("region", None),
        P(),
        P(),
        P(),
        P(),
        P(),
        P(),
        P(),
        P("noise", "region", None),
    )
    out_specs = (P("noise", "region", None), P())
    return jax.shard_map(body, mesh=mesh, in_specs=in_specs, out_specs=out_specs, check_vma=False)
```

time: 76.8 us -> 67.9 us (0.88)
  Pallas kernels: 70.9 us -> 66.4 us
  local copies, waits for them, and re-layouts: 2.22 us -> 0 us
  other arithmetic: 2.19 us -> 0 us
    pallas_call x1, Pallas kernels: 70.9 us -> 64.4 us  [body(): pl.pallas_call(kernel, out_shape=(jax.ShapeDtypeStruct((NODES, D), BF), j...]
    unnamed x4 -> x0, local copies, waits for them, and re-layouts: 2.22 us -> none
    convert_element_type x1 -> x0, other arithmetic: 2.19 us -> none  [body(): return (mesh_out[None], grad.astype(F32))]
    pallas_call x0 -> x1, Pallas kernels: none -> 2.06 us  [body(): pl.pallas_call(widen, out_shape=(jax.ShapeDtypeStruct((1, NODES, D), BF),...]
where the time goes in v2:
time: 67.9 us; the launch traced here: 67.7 us
  Pallas kernels  66.4 us (98%)
  between operations  1.29 us (2%)
    pallas_call x1, Pallas kernels, body(): pl.pallas_call(kernel, out_shape=(jax.ShapeDtypeStruct((NODES, D), BF), j...  64.4 us
    pallas_call x1, Pallas kernels, body(): pl.pallas_call(widen, out_shape=(jax.ShapeDtypeStruct((1, NODES, D), BF),...  2.06 us

profile of v2, /device:TPU:1, one launch (start us, length us, event | category | flops | bytes accessed | tf_op | source)
XLA Modules:
  0.0 67.7 jit_solution(2594132981732501418)
XLA Ops:
  1.3 64.4 %shard_map.176 = (bf16[256,512]{1,0:T(8,128)(2,1)}, bf16[512,512]{1,0:T(8,128)(2,1)}) custom-call(s32[1,1]{1,0:T(1,128)} %bitcast.6.level_ref, s32[1,32,128]{2,1,0:T(8,128)} %send_hbm.1, s32[32,128]{1,0:T(8,128)} %bitcast.8, s32[32,128]{1,0:T(8,128)} %bitcast.9, s32[32,256]{1,0:T(8,128)} %bitcast.7, bf16[84,2048]{1,0:T(8,128)(2,1)} %target_hbm.1, ...), custom_call_target="tpu_custom_call" | custom-call | flops 12000000000 | bytes 6000000 | tf_op jit(solution)/shard_map/pallas_call | solution.py:637
  65.7 2.1 %shard_map.177 = (bf16[1,256,512]{2,1,0:T(8,128)(2,1)}, f32[512,512]{1,0:T(8,128)}) custom-call(bf16[256,512]{1,0:T(8,128)(2,1)} %get-tuple-element.4.mesh_hbm, bf16[512,512]{1,0:T(8,128)(2,1)} %get-tuple-element.5.grad_hbm), custom_call_target="tpu_custom_call" | custom-call | tf_op jit(solution)/shard_map/pallas_call | solution.py:657

commit v3 on v2

--- a/solution.py
+++ b/solution.py
@@ -28,7 +28,8 @@
 ROWS = 4
 XS = 4
 ETILE = 512
-HSPLIT = 8
+HSPLIT = 1
+PIECE = 32
 HALF = GRID // 2
 KCAT = 128
 
@@ -44,6 +45,11 @@
 AROUND = sorted(
     [(dx, dy) for dx in range(XS) for dy in range(ROWS) if dx or dy],
     key=lambda d: (-min(d[0], XS - d[0]) - min(d[1], ROWS - d[1]), d),
+)
+
+COLUMN = sorted(
+    [(dy, dz) for dy in range(ROWS) for dz in range(PLANES) if dy or dz],
+    key=lambda d: (-min(d[0], ROWS - d[0]) - min(d[1], PLANES - d[1]), d),
 )
 
 NT = (((1,), (1,)), ((), ()))
@@ -105,8 +111,8 @@
     qkv_hbm,
     ow_hbm,
     cot_hbm,
-    mesh_out_ref,
-    grad_ref,
+    mesh_out_hbm,
+    grad_hbm,
     send_v,
     esrc_v,
     edst_v,
@@ -155,6 +161,7 @@
     rb2,
     zbuf,
     fbuf,
+    mout_v,
     s1_send,
     s1_recv,
     s2_send,
@@ -165,6 +172,7 @@
     g2_recv,
     g1_send,
     g1_recv,
+    out_sem,
 ):
     noise = lax.axis_index("noise")
     me = lax.axis_index("region")
@@ -182,8 +190,11 @@
             "region": mz * ROWS + lax.rem(my + dy, ROWS),
         }
 
+    def region_at(dy, dz):
+        return lax.rem(mz + dz, PLANES) * ROWS + lax.rem(my + dy, ROWS)
+
     def piece(x, y):
-        return pl.ds(pl.multiple_of((x * ROWS + y) * 16, 16), 16)
+        return pl.ds(pl.multiple_of((x * ROWS + y) * PIECE, PIECE), PIECE)
 
     pairs = [
         (noise_hbm.at[0], noise_v),
@@ -232,11 +243,8 @@
             barrier, inc=1, device_id=device, device_id_type=pl.DeviceIdType.MESH
         )
 
-    def tell_region(i, carry):
-        tell({"region": lax.rem(me + i, REGIONS)})
-        return carry
-
-    lax.fori_loop(1, REGIONS, tell_region, 0)
+    for dy, dz in COLUMN:
+        tell({"region": region_at(dy, dz)})
     beyond = [(dx, dy) for dx, dy in AROUND if dx]
     for dx, dy in beyond:
         tell(across(dx, dy))
@@ -260,10 +268,7 @@
         ) * scale
         g_v[part * VPAD : part * VPAD + VARS, :] = noised.astype(BF)
     ld_send.wait()
-    pl.semaphore_wait(barrier, REGIONS - 1 + len(beyond) + 1)
-
-    def send_plane(i, carry):
-        z = lax.rem(mz + plane_offset(i), PLANES)
+    def pick_plane(z):
         idx = lanes(send_v, ROWS * z, ROWS)
         upper = idx >= HALF
         low = jnp.where(upper, idx - HALF, idx).astype(F32)
@@ -273,8 +278,11 @@
         both = dot(g_v[...], hot)
         picked = jnp.where(upper, both[VPAD:, :], both[:VPAD, :]).astype(BF)
         for k in range(ROWS):
+            sbuf[ROWS * z + k] = picked[:VARS, k * SLOT : (k + 1) * SLOT]
+
+    def copy_plane(z):
+        for k in range(ROWS):
             r = ROWS * z + k
-            sbuf[r] = picked[:VARS, k * SLOT : (k + 1) * SLOT]
 
             @pl.when(r != me)
             def _():
@@ -291,10 +299,17 @@
             def _():
                 pltpu.make_async_copy(sbuf.at[r], rbuf.at[me], a2a_recv.at[mz]).start()
 
+    def send_plane(i, carry):
+        z = lax.rem(mz + plane_offset(i), PLANES)
+        pick_plane(z)
+        copy_plane(z)
         return carry
 
     with jax.named_scope("send_columns"):
-        lax.fori_loop(0, PLANES, send_plane, 0)
+        pick_plane(lax.rem(mz + 4, PLANES))
+        pl.semaphore_wait(barrier, REGIONS - 1 + len(beyond) + 1)
+        copy_plane(lax.rem(mz + 4, PLANES))
+        lax.fori_loop(1, PLANES, send_plane, 0)
 
     with jax.named_scope("tables"):
         ld_esrc.wait()
@@ -359,8 +374,8 @@
         for e in range(EDGES // ETILE):
             cols = slice(e * ETILE, (e + 1) * ETILE)
             x = dot(wt_v[...], acc_v[:, cols])
-            half = 0.5 * x
-            hid_v[:, cols] = (half + half * jnp.tanh(half)).astype(BF)
+            half = (0.5 * x).astype(BF)
+            hid_v[:, cols] = half + half * jnp.tanh(half)
         hidden_sum = dot_nt(node_v[...], hid_v[...])
 
     with jax.named_scope("encode"):
@@ -409,54 +424,69 @@
             for h in range(HEADS)
         ]
 
+    other = pl.ds(pl.multiple_of((1 - core) * NODES, NODES), NODES)
+    mine = pl.ds(pl.multiple_of(core * NODES, NODES), NODES)
+    swaps = []
     with jax.named_scope("attention_halo"):
         halo_got.wait()
-        beside = dot(halo_v[...], qkv_v[:, D:])
-        key = units(beside[:, :D])
-        value = beside[:, D:].astype(BF)
-        for h in range(HEADS):
-            both = mixed[h] + mix(
-                query[h], key[h], value[:, h * HEAD : (h + 1) * HEAD], count_h[...]
+        ld_cot.wait()
+        for pair in range(2):
+            wide = 2 * HEAD
+            beside = dot(halo_v[...], qkv_v[:, D + pair * wide : D + (pair + 1) * wide])
+            value = dot(
+                halo_v[...], qkv_v[:, 2 * D + pair * wide : 2 * D + (pair + 1) * wide]
+            ).astype(BF)
+            for h in range(2):
+                head = 2 * pair + h
+                cols = slice(h * HEAD, (h + 1) * HEAD)
+                key = rms(beside[:, cols], head_eps).astype(BF)
+                both = mixed[head] + mix(query[head], key, value[:, cols], count_h[...])
+                att_v[:, head * HEAD : (head + 1) * HEAD] = both[:, :HEAD] / both[:, HEAD:]
+            rows = slice(pair * wide, (pair + 1) * wide)
+            attt_v[rows, :] = att_v[:, rows].T.astype(BF)
+            sb1[rows, :] = dot(attt_v[rows, :], cot_v[:, other]).astype(BF)
+            swap = pltpu.make_async_remote_copy(
+                src_ref=sb1.at[rows],
+                dst_ref=rb1.at[rows],
+                send_sem=s1_send.at[pair],
+                recv_sem=s1_recv.at[pair],
+                device_id={"noise": partner},
+                device_id_type=pl.DeviceIdType.MESH,
             )
-            att_v[:, h * HEAD : (h + 1) * HEAD] = both[:, :HEAD] / both[:, HEAD:]
-        attt_v[...] = att_v[...].T.astype(BF)
-
-    with jax.named_scope("gradient_term"):
-        ld_cot.wait()
-        other = pl.multiple_of((1 - core) * NODES, NODES)
-        mine = pl.multiple_of(core * NODES, NODES)
-        sb1[...] = dot(attt_v[pl.ds(other, NODES), :], cot_v[...]).astype(BF)
-        swap = pltpu.make_async_remote_copy(
-            src_ref=sb1,
-            dst_ref=rb1,
-            send_sem=s1_send,
-            recv_sem=s1_recv,
-            device_id={"noise": partner},
-            device_id_type=pl.DeviceIdType.MESH,
-        )
-        swap.start()
-        p_v[...] = dot(attt_v[pl.ds(mine, NODES), :], cot_v[...])
-        swap.wait_recv()
+            swap.start()
+            swaps.append(swap)
+            p_v[rows, :] = dot(attt_v[rows, :], cot_v[:, mine])
 
     with jax.named_scope("reduce_xy"):
-        p_v[...] = p_v[...] + rb1[...].astype(F32)
-        sb2[...] = p_v[...].astype(BF)
-        for i, (dx, dy) in enumerate(AROUND):
-            there = piece(lax.rem(mx + dx, XS), lax.rem(my + dy, ROWS))
-            pltpu.make_async_remote_copy(
-                src_ref=sb2.at[there],
-                dst_ref=rb2.at[i],
-                send_sem=s2_send,
-                recv_sem=s2_recv,
-                device_id=across(dx, dy),
-                device_id_type=pl.DeviceIdType.MESH,
-            ).start()
+        for pair in range(2):
+            swaps[pair].wait_recv()
+            rows = slice(pair * 2 * HEAD, (pair + 1) * 2 * HEAD)
+            total = p_v[rows, :] + rb1[rows, :].astype(F32)
+            p_v[rows, :] = total
+            sb2[rows, :] = total.astype(BF)
+            for x in (2 * pair, 2 * pair + 1):
+                for dy in (2, 1, 3, 0):
+
+                    @pl.when((x != mx) | (dy != 0))
+                    def _():
+                        slot = lax.rem(mx + XS - x, XS) * ROWS + (ROWS - dy) % ROWS - 1
+                        pltpu.make_async_remote_copy(
+                            src_ref=sb2.at[piece(x, lax.rem(my + dy, ROWS))],
+                            dst_ref=rb2.at[slot],
+                            send_sem=s2_send,
+                            recv_sem=s2_recv,
+                            device_id={
+                                "noise": x * 2 + core,
+                                "region": mz * ROWS + lax.rem(my + dy, ROWS),
+                            },
+                            device_id_type=pl.DeviceIdType.MESH,
+                        ).start()
 
     with jax.named_scope("mesh_out"):
         ld_ow.wait()
-        mesh_out_ref[...] = (
-            enc_v[...] + dot(att_v[...].astype(BF), ow_v[...])
-        ).astype(BF)
+        mout_v[...] = (enc_v[...] + dot(att_v[...].astype(BF), ow_v[...])).astype(BF)
+        mesh_out = pltpu.make_async_copy(mout_v, mesh_out_hbm, out_sem.at[2 * XS])
+        mesh_out.start()
 
     with jax.named_scope("reduce_z"):
         pltpu.make_async_copy(rb2, rb2, s2_recv).wait()
@@ -480,62 +510,86 @@
             total = total + zbuf[z].astype(F32)
 
     with jax.named_scope("gather_xy"):
-        place = pl.ds(
-            pl.multiple_of(core * NODES + (mx * ROWS + my) * 16, 16), 16
-        )
-        fbuf[place, :] = total.astype(BF)
+        place = piece(mx, my)
+        fbuf[core, place, :] = total.astype(BF)
         for dx, dy in AROUND:
             pltpu.make_async_remote_copy(
-                src_ref=fbuf.at[place],
-                dst_ref=fbuf.at[place],
+                src_ref=fbuf.at[core, place],
+                dst_ref=fbuf.at[core, place],
                 send_sem=g2_send,
-                recv_sem=g2_recv,
+                recv_sem=g2_recv.at[dx],
                 device_id=across(dx, dy),
                 device_id_type=pl.DeviceIdType.MESH,
             ).start()
-        pltpu.make_async_copy(rb2, rb2, g2_recv).wait()
 
     with jax.named_scope("gather_core"):
-        half = pl.ds(mine, NODES)
-        back = pltpu.make_async_remote_copy(
-            src_ref=fbuf.at[half],
-            dst_ref=fbuf.at[half],
-            send_sem=g1_send,
-            recv_sem=g1_recv,
-            device_id={"noise": partner},
-            device_id_type=pl.DeviceIdType.MESH,
-        )
-        back.start()
-        back.wait_recv()
-        grad_ref[...] = fbuf[...]
+        backs, outs = [], []
+        for i, dx in enumerate((0, 1, 3, 2)):
+            some = rb2.at[0 : ROWS - (dx == 0)]
+            pltpu.make_async_copy(some, some, g2_recv.at[dx]).wait()
+            rows = pl.ds(
+                pl.multiple_of(lax.rem(mx + XS - dx, XS) * ROWS * PIECE, ROWS * PIECE),
+                ROWS * PIECE,
+            )
+            back = pltpu.make_async_remote_copy(
+                src_ref=fbuf.at[core, rows],
+                dst_ref=fbuf.at[core, rows],
+                send_sem=g1_send.at[i],
+                recv_sem=g1_recv.at[i],
+                device_id={"noise": partner},
+                device_id_type=pl.DeviceIdType.MESH,
+            )
+            back.start()
+            backs.append(back)
+            out = pltpu.make_async_copy(
+                fbuf.at[core, rows], grad_hbm.at[core, rows], out_sem.at[i]
+            )
+            out.start()
+            outs.append((rows, out))
+        for i in range(XS):
+            backs[i].wait_recv()
+            rows, out = outs[i]
+            out = pltpu.make_async_copy(
+                fbuf.at[1 - core, rows], grad_hbm.at[1 - core, rows], out_sem.at[XS + i]
+            )
+            out.start()
+            outs.append((rows, out))
 
     sent = sbuf.at[0 : REGIONS - 1]
     pltpu.make_async_copy(sent, sent, a2a_send).wait()
     halo_sent.wait()
-    swap.wait_send()
+    for swap in swaps:
+        swap.wait_send()
     pltpu.make_async_copy(rb2, rb2, s2_send).wait()
     pltpu.make_async_copy(seven, seven, s3_send).wait()
     pltpu.make_async_copy(rb2, rb2, g2_send).wait()
-    back.wait_send()
+    mesh_out.wait()
+    for back in backs:
+        back.wait_send()
+    for _, out in outs:
+        out.wait()
 
 
 def widen(mesh_hbm, grad_hbm, mesh_out_hbm, grad_out_hbm, narrow, wide, mesh_v, in_sems, out_sems):
-    parts = [pl.ds(i * 128, 128) for i in range(4)]
+    parts = [(c, slice(i * 128, (i + 1) * 128)) for i in range(4) for c in range(2)]
     got = [
-        pltpu.make_async_copy(grad_hbm.at[p], narrow.at[p], in_sems.at[i])
-        for i, p in enumerate(parts)
+        pltpu.make_async_copy(grad_hbm.at[c, rows], narrow.at[c, rows], in_sems.at[i])
+        for i, (c, rows) in enumerate(parts)
     ]
-    mesh_got = pltpu.make_async_copy(mesh_hbm, mesh_v, in_sems.at[4])
+    mesh_got = pltpu.make_async_copy(mesh_hbm, mesh_v, in_sems.at[8])
     for copy in got:
         copy.start()
     mesh_got.start()
     sent = []
-    for i, p in enumerate(parts):
+    for i, (c, rows) in enumerate(parts):
         got[i].wait()
-        wide[p, :] = narrow[p, :].astype(F32)
-        copy = pltpu.make_async_copy(wide.at[p], grad_out_hbm.at[p], out_sems.at[i])
-        copy.start()
-        sent.append(copy)
+        wide[rows, c * NODES : (c + 1) * NODES] = narrow[c, rows, :].astype(F32)
+        if c == 1:
+            copy = pltpu.make_async_copy(
+                wide.at[rows], grad_out_hbm.at[rows], out_sems.at[i // 2]
+            )
+            copy.start()
+            sent.append(copy)
     mesh_got.wait()
     copy = pltpu.make_async_copy(mesh_v, mesh_out_hbm.at[0], out_sems.at[4])
     copy.start()
@@ -626,26 +680,26 @@
         dma((PLANES,)),
         dma,
         dma,
-        vmem((NODES, D), F32),
+        vmem((D, NODES), F32),
+        vmem((D, NODES), BF),
+        vmem((D, NODES), BF),
+        vmem((D, NODES), BF),
+        vmem((len(AROUND), PIECE, NODES), BF),
+        vmem((PLANES, PIECE, NODES), BF),
+        vmem((2, D, NODES), BF),
         vmem((NODES, D), BF),
-        vmem((NODES, D), BF),
-        vmem((NODES, D), BF),
-        vmem((len(AROUND), 16, D), BF),
-        vmem((PLANES, 16, D), BF),
-        vmem((D, D), BF),
-    ] + [dma] * 10
+        dma((2,)),
+        dma((2,)),
+    ] + [dma] * 5 + [dma((XS,))] * 3 + [dma((2 * XS + 1,))]
     mesh_out, grad = pl.pallas_call(
         kernel,
         out_shape=(
             jax.ShapeDtypeStruct((NODES, D), BF),
-            jax.ShapeDtypeStruct((D, D), BF),
+            jax.ShapeDtypeStruct((2, D, NODES), BF),
         ),
         in_specs=[pl.BlockSpec(memory_space=pltpu.VMEM)]
         + [pl.BlockSpec(memory_space=pl.ANY)] * (len(operands) - 1),
-        out_specs=(
-            pl.BlockSpec(memory_space=pltpu.VMEM),
-            pl.BlockSpec(memory_space=pltpu.VMEM),
-        ),
+        out_specs=[pl.BlockSpec(memory_space=pl.ANY)] * 2,
         scratch_shapes=scratch,
         compiler_params=pltpu.CompilerParams(
             collective_id=0, has_side_effects=True, vmem_limit_bytes=60 * 1024 * 1024
@@ -663,10 +717,10 @@
         in_specs=[pl.BlockSpec(memory_space=pl.ANY)] * 2,
         out_specs=[pl.BlockSpec(memory_space=pl.ANY)] * 2,
         scratch_shapes=[
-            vmem((D, D), BF),
+            vmem((2, D, NODES), BF),
             vmem((D, D), F32),
             vmem((NODES, D), BF),
-            dma((5,)),
+            dma((9,)),
             dma((5,)),
         ],
     )(mesh_out, grad)

time: 67.9 us -> 66.3 us (0.976)
  Pallas kernels: 66.4 us -> 64.8 us
    pallas_call x1, Pallas kernels: 64.4 us -> 62.8 us  [body(): pl.pallas_call(kernel, out_shape=(jax.ShapeDtypeStruct((NODES, D), BF), j...]
where the time goes in v3:
time: 66.3 us; the launch traced here: 66.1 us
  Pallas kernels  64.8 us (98%)
  between operations  1.29 us (2%)
    pallas_call x1, Pallas kernels, body(): pl.pallas_call(kernel, out_shape=(jax.ShapeDtypeStruct((NODES, D), BF), j...  62.8 us
    pallas_call x1, Pallas kernels, body(): pl.pallas_call(widen, out_shape=(jax.ShapeDtypeStruct((1, NODES, D), BF),...  2.05 us

profile of v3, /device:TPU:1, one launch (start us, length us, event | category | flops | bytes accessed | tf_op | source)
XLA Modules:
  0.0 66.1 jit_solution(18230020466921979751)
XLA Ops:
  1.3 62.8 %shard_map.176 = (bf16[256,512]{1,0:T(8,128)(2,1)}, bf16[2,512,256]{2,1,0:T(8,128)(2,1)}) custom-call(s32[1,1]{1,0:T(1,128)} %bitcast.6.level_ref, s32[1,32,128]{2,1,0:T(8,128)} %send_hbm.1, s32[32,128]{1,0:T(8,128)} %bitcast.8, s32[32,128]{1,0:T(8,128)} %bitcast.9, s32[32,256]{1,0:T(8,128)} %bitcast.7, bf16[84,2048]{1,0:T(8,128)(2,1)} %target_hbm.1, ...), custom_call_target="tpu_custom_call" | custom-call | flops 12000000000 | bytes 6000000 | tf_op jit(solution)/shard_map/pallas_call | solution.py:694
  64.1 2.1 %shard_map.177 = (bf16[1,256,512]{2,1,0:T(8,128)(2,1)}, f32[512,512]{1,0:T(8,128)}) custom-call(bf16[256,512]{1,0:T(8,128)(2,1)} %get-tuple-element.4.mesh_hbm, bf16[2,512,256]{2,1,0:T(8,128)(2,1)} %get-tuple-element.5.grad_hbm), custom_call_target="tpu_custom_call" | custom-call | tf_op jit(solution)/shard_map/pallas_call | solution.py:711

commit v4 on v3

--- a/solution.py
+++ b/solution.py
@@ -193,6 +193,9 @@
     def region_at(dy, dz):
         return lax.rem(mz + dz, PLANES) * ROWS + lax.rem(my + dy, ROWS)
 
+    def sixteen(pair, x, y):
+        return pl.ds(pl.multiple_of(pair * NODES + (x * ROWS + y) * 16, 16), 16)
+
     def piece(x, y):
         return pl.ds(pl.multiple_of((x * ROWS + y) * PIECE, PIECE), PIECE)
 
@@ -281,8 +284,8 @@
             sbuf[ROWS * z + k] = picked[:VARS, k * SLOT : (k + 1) * SLOT]
 
     def copy_plane(z):
-        for k in range(ROWS):
-            r = ROWS * z + k
+        for k, l in ((0, 3), (3, 0), (1, 2), (2, 1)):
+            r = ROWS * z + jnp.where(lax.rem(z, 2) == 0, k, l)
 
             @pl.when(r != me)
             def _():
@@ -427,6 +430,24 @@
     other = pl.ds(pl.multiple_of((1 - core) * NODES, NODES), NODES)
     mine = pl.ds(pl.multiple_of(core * NODES, NODES), NODES)
     swaps = []
+
+    def send_pieces(pair):
+        swaps[pair].wait_recv()
+        rows = slice(pair * 2 * HEAD, (pair + 1) * 2 * HEAD)
+        total = p_v[rows, :] + rb1[rows, :].astype(F32)
+        p_v[rows, :] = total
+        sb2[rows, :] = total.astype(BF)
+        for i, (dx, dy) in enumerate(AROUND):
+            there = sixteen(pair, lax.rem(mx + dx, XS), lax.rem(my + dy, ROWS))
+            pltpu.make_async_remote_copy(
+                src_ref=sb2.at[there],
+                dst_ref=rb2.at[i, pair * 16 : (pair + 1) * 16],
+                send_sem=s2_send,
+                recv_sem=s2_recv,
+                device_id=across(dx, dy),
+                device_id_type=pl.DeviceIdType.MESH,
+            ).start()
+
     with jax.named_scope("attention_halo"):
         halo_got.wait()
         ld_cot.wait()
@@ -442,6 +463,8 @@
                 key = rms(beside[:, cols], head_eps).astype(BF)
                 both = mixed[head] + mix(query[head], key, value[:, cols], count_h[...])
                 att_v[:, head * HEAD : (head + 1) * HEAD] = both[:, :HEAD] / both[:, HEAD:]
+            if pair == 1:
+                send_pieces(0)
             rows = slice(pair * wide, (pair + 1) * wide)
             attt_v[rows, :] = att_v[:, rows].T.astype(BF)
             sb1[rows, :] = dot(attt_v[rows, :], cot_v[:, other]).astype(BF)
@@ -458,29 +481,7 @@
             p_v[rows, :] = dot(attt_v[rows, :], cot_v[:, mine])
 
     with jax.named_scope("reduce_xy"):
-        for pair in range(2):
-            swaps[pair].wait_recv()
-            rows = slice(pair * 2 * HEAD, (pair + 1) * 2 * HEAD)
-            total = p_v[rows, :] + rb1[rows, :].astype(F32)
-            p_v[rows, :] = total
-            sb2[rows, :] = total.astype(BF)
-            for x in (2 * pair, 2 * pair + 1):
-                for dy in (2, 1, 3, 0):
-
-                    @pl.when((x != mx) | (dy != 0))
-                    def _():
-                        slot = lax.rem(mx + XS - x, XS) * ROWS + (ROWS - dy) % ROWS - 1
-                        pltpu.make_async_remote_copy(
-                            src_ref=sb2.at[piece(x, lax.rem(my + dy, ROWS))],
-                            dst_ref=rb2.at[slot],
-                            send_sem=s2_send,
-                            recv_sem=s2_recv,
-                            device_id={
-                                "noise": x * 2 + core,
-                                "region": mz * ROWS + lax.rem(my + dy, ROWS),
-                            },
-                            device_id_type=pl.DeviceIdType.MESH,
-                        ).start()
+        send_pieces(1)
 
     with jax.named_scope("mesh_out"):
         ld_ow.wait()
@@ -490,7 +491,7 @@
 
     with jax.named_scope("reduce_z"):
         pltpu.make_async_copy(rb2, rb2, s2_recv).wait()
-        total = p_v[piece(mx, my), :]
+        total = jnp.concatenate([p_v[sixteen(pair, mx, my), :] for pair in range(2)], axis=0)
         for i in range(len(AROUND)):
             total = total + rb2[i].astype(F32)
         zbuf[mz] = total.astype(BF)
@@ -583,15 +584,23 @@
     sent = []
     for i, (c, rows) in enumerate(parts):
         got[i].wait()
-        wide[rows, c * NODES : (c + 1) * NODES] = narrow[c, rows, :].astype(F32)
+        for q in range(4):
+            for pair in range(2):
+                first = rows.start + q * PIECE + pair * 16
+                to = pair * NODES + (rows.start // PIECE + q) * 16
+                wide[to : to + 16, c * NODES : (c + 1) * NODES] = narrow[
+                    c, first : first + 16, :
+                ].astype(F32)
         if c == 1:
-            copy = pltpu.make_async_copy(
-                wide.at[rows], grad_out_hbm.at[rows], out_sems.at[i // 2]
-            )
-            copy.start()
-            sent.append(copy)
+            for pair in range(2):
+                block = pl.ds(pair * NODES + rows.start // 2, 64)
+                copy = pltpu.make_async_copy(
+                    wide.at[block], grad_out_hbm.at[block], out_sems.at[i - 1 + pair]
+                )
+                copy.start()
+                sent.append(copy)
     mesh_got.wait()
-    copy = pltpu.make_async_copy(mesh_v, mesh_out_hbm.at[0], out_sems.at[4])
+    copy = pltpu.make_async_copy(mesh_v, mesh_out_hbm.at[0], out_sems.at[8])
     copy.start()
     for copy in sent + [copy]:
         copy.wait()
@@ -721,7 +730,7 @@
             vmem((D, D), F32),
             vmem((NODES, D), BF),
             dma((9,)),
-            dma((5,)),
+            dma((9,)),
         ],
     )(mesh_out, grad)
     return mesh_out, grad

time: 66.3 us -> 64.7 us (0.976)
  Pallas kernels: 64.8 us -> 63.2 us
    pallas_call x1, Pallas kernels: 62.8 us -> 61.2 us  [body(): pl.pallas_call(kernel, out_shape=(jax.ShapeDtypeStruct((NODES, D), BF), j...]
where the time goes in v4:
time: 64.7 us; the launch traced here: 64.5 us
  Pallas kernels  63.2 us (98%)
  between operations  1.29 us (2%)
    pallas_call x1, Pallas kernels, body(): pl.pallas_call(kernel, out_shape=(jax.ShapeDtypeStruct((NODES, D), BF), j...  61.2 us
    pallas_call x1, Pallas kernels, body(): pl.pallas_call(widen, out_shape=(jax.ShapeDtypeStruct((1, NODES, D), BF),...  2.08 us

profile of v4, /device:TPU:1, one launch (start us, length us, event | category | flops | bytes accessed | tf_op | source)
XLA Modules:
  0.0 64.5 jit_solution(5518943643144723572)
XLA Ops:
  1.3 61.2 %shard_map.176 = (bf16[256,512]{1,0:T(8,128)(2,1)}, bf16[2,512,256]{2,1,0:T(8,128)(2,1)}) custom-call(s32[1,1]{1,0:T(1,128)} %bitcast.6.level_ref, s32[1,32,128]{2,1,0:T(8,128)} %send_hbm.1, s32[32,128]{1,0:T(8,128)} %bitcast.8, s32[32,128]{1,0:T(8,128)} %bitcast.9, s32[32,256]{1,0:T(8,128)} %bitcast.7, bf16[84,2048]{1,0:T(8,128)(2,1)} %target_hbm.1, ...), custom_call_target="tpu_custom_call" | custom-call | flops 12000000000 | bytes 6000000 | tf_op jit(solution)/shard_map/pallas_call | solution.py:703
  62.5 2.1 %shard_map.177 = (bf16[1,256,512]{2,1,0:T(8,128)(2,1)}, f32[512,512]{1,0:T(8,128)}) custom-call(bf16[256,512]{1,0:T(8,128)(2,1)} %get-tuple-element.4.mesh_hbm, bf16[2,512,256]{2,1,0:T(8,128)(2,1)} %get-tuple-element.5.grad_hbm), custom_call_target="tpu_custom_call" | custom-call | tf_op jit(solution)/shard_map/pallas_call | solution.py:720

commit v5 on v4

--- a/solution.py
+++ b/solution.py
@@ -89,8 +89,10 @@
 
 
 def plane_offset(i):
-    half = lax.div(i + 1, 2)
-    return lax.rem(4 + half * (1 - 2 * lax.rem(i, 2)) + PLANES, PLANES)
+    half = lax.div(i, 2) + 1
+    return jnp.where(
+        i == PLANES - 1, 0, jnp.where(lax.rem(i, 2) == 0, half, PLANES - half)
+    )
 
 
 def kernel(
@@ -309,9 +311,9 @@
         return carry
 
     with jax.named_scope("send_columns"):
-        pick_plane(lax.rem(mz + 4, PLANES))
+        pick_plane(lax.rem(mz + 1, PLANES))
         pl.semaphore_wait(barrier, REGIONS - 1 + len(beyond) + 1)
-        copy_plane(lax.rem(mz + 4, PLANES))
+        copy_plane(lax.rem(mz + 1, PLANES))
         lax.fori_loop(1, PLANES, send_plane, 0)
 
     with jax.named_scope("tables"):
@@ -352,7 +354,7 @@
         count_h[:, HALO:] = count_t[HALO + NODES :, :].T
 
     def gather_plane(i, carry):
-        z = lax.rem(mz + PLANES - plane_offset(i), PLANES)
+        z = lax.rem(mz + PLANES - plane_offset(lax.rem(i + PLANES - 1, PLANES)), PLANES)
         window = rbuf.at[pl.ds(ROWS * z, ROWS)]
         pltpu.make_async_copy(window, window, a2a_recv.at[z]).wait()
         for k in range(ROWS):
@@ -443,7 +445,7 @@
                 src_ref=sb2.at[there],
                 dst_ref=rb2.at[i, pair * 16 : (pair + 1) * 16],
                 send_sem=s2_send,
-                recv_sem=s2_recv,
+                recv_sem=s2_recv.at[pair],
                 device_id=across(dx, dy),
                 device_id_type=pl.DeviceIdType.MESH,
             ).start()
@@ -489,39 +491,45 @@
         mesh_out = pltpu.make_async_copy(mout_v, mesh_out_hbm, out_sem.at[2 * XS])
         mesh_out.start()
 
+    lots = [pl.ds(pair * 16, 16) for pair in range(2)]
     with jax.named_scope("reduce_z"):
-        pltpu.make_async_copy(rb2, rb2, s2_recv).wait()
-        total = jnp.concatenate([p_v[sixteen(pair, mx, my), :] for pair in range(2)], axis=0)
-        for i in range(len(AROUND)):
-            total = total + rb2[i].astype(F32)
-        zbuf[mz] = total.astype(BF)
-        for d in (4, 3, 5, 2, 6, 1, 7):
-            pltpu.make_async_remote_copy(
-                src_ref=zbuf.at[mz],
-                dst_ref=zbuf.at[mz],
-                send_sem=s3_send,
-                recv_sem=s3_recv,
-                device_id={"region": lax.rem(me + ROWS * d, REGIONS)},
-                device_id_type=pl.DeviceIdType.MESH,
-            ).start()
-        seven = zbuf.at[0 : PLANES - 1]
-        pltpu.make_async_copy(seven, seven, s3_recv).wait()
-        total = zbuf[0].astype(F32)
-        for z in range(1, PLANES):
-            total = total + zbuf[z].astype(F32)
+        for pair, lot in enumerate(lots):
+            window = rb2.at[:, lot]
+            pltpu.make_async_copy(window, window, s2_recv.at[pair]).wait()
+            total = p_v[sixteen(pair, mx, my), :]
+            for i in range(len(AROUND)):
+                total = total + rb2[i, lot].astype(F32)
+            zbuf[mz, lot] = total.astype(BF)
+            for d in (4, 3, 5, 2, 6, 1, 7):
+                pltpu.make_async_remote_copy(
+                    src_ref=zbuf.at[mz, lot],
+                    dst_ref=zbuf.at[mz, lot],
+                    send_sem=s3_send,
+                    recv_sem=s3_recv.at[pair],
+                    device_id={"region": lax.rem(me + ROWS * d, REGIONS)},
+                    device_id_type=pl.DeviceIdType.MESH,
+                ).start()
 
     with jax.named_scope("gather_xy"):
-        place = piece(mx, my)
-        fbuf[core, place, :] = total.astype(BF)
-        for dx, dy in AROUND:
-            pltpu.make_async_remote_copy(
-                src_ref=fbuf.at[core, place],
-                dst_ref=fbuf.at[core, place],
-                send_sem=g2_send,
-                recv_sem=g2_recv.at[dx],
-                device_id=across(dx, dy),
-                device_id_type=pl.DeviceIdType.MESH,
-            ).start()
+        for pair, lot in enumerate(lots):
+            window = zbuf.at[0 : PLANES - 1, lot]
+            pltpu.make_async_copy(window, window, s3_recv.at[pair]).wait()
+            total = zbuf[0, lot].astype(F32)
+            for z in range(1, PLANES):
+                total = total + zbuf[z, lot].astype(F32)
+            place = pl.ds(
+                pl.multiple_of((mx * ROWS + my) * PIECE + pair * 16, 16), 16
+            )
+            fbuf[core, place, :] = total.astype(BF)
+            for dx, dy in AROUND:
+                pltpu.make_async_remote_copy(
+                    src_ref=fbuf.at[core, place],
+                    dst_ref=fbuf.at[core, place],
+                    send_sem=g2_send,
+                    recv_sem=g2_recv.at[dx],
+                    device_id=across(dx, dy),
+                    device_id_type=pl.DeviceIdType.MESH,
+                ).start()
 
     with jax.named_scope("gather_core"):
         backs, outs = [], []
@@ -562,6 +570,7 @@
     for swap in swaps:
         swap.wait_send()
     pltpu.make_async_copy(rb2, rb2, s2_send).wait()
+    seven = zbuf.at[0 : PLANES - 1]
     pltpu.make_async_copy(seven, seven, s3_send).wait()
     pltpu.make_async_copy(rb2, rb2, g2_send).wait()
     mesh_out.wait()
@@ -699,7 +708,7 @@
         vmem((NODES, D), BF),
         dma((2,)),
         dma((2,)),
-    ] + [dma] * 5 + [dma((XS,))] * 3 + [dma((2 * XS + 1,))]
+    ] + [dma, dma((2,)), dma, dma((2,)), dma] + [dma((XS,))] * 3 + [dma((2 * XS + 1,))]
     mesh_out, grad = pl.pallas_call(
         kernel,
         out_shape=(

time: 64.7 us -> 63.5 us (0.981)
  Pallas kernels: 63.2 us -> 62.1 us
    pallas_call x1, Pallas kernels: 61.2 us -> 60 us  [body(): pl.pallas_call(kernel, out_shape=(jax.ShapeDtypeStruct((NODES, D), BF), j...]
where the time goes in v5:
time: 63.5 us; the launch traced here: 63.4 us
  Pallas kernels  62.1 us (98%)
  between operations  1.29 us (2%)
    pallas_call x1, Pallas kernels, body(): pl.pallas_call(kernel, out_shape=(jax.ShapeDtypeStruct((NODES, D), BF), j...  60 us
    pallas_call x1, Pallas kernels, body(): pl.pallas_call(widen, out_shape=(jax.ShapeDtypeStruct((1, NODES, D), BF),...  2.08 us

profile of v5, /device:TPU:1, one launch (start us, length us, event | category | flops | bytes accessed | tf_op | source)
XLA Modules:
  0.0 63.4 jit_solution(14421850374925630609)
XLA Ops:
  1.3 60.0 %shard_map.176 = (bf16[256,512]{1,0:T(8,128)(2,1)}, bf16[2,512,256]{2,1,0:T(8,128)(2,1)}) custom-call(s32[1,1]{1,0:T(1,128)} %bitcast.6.level_ref, s32[1,32,128]{2,1,0:T(8,128)} %send_hbm.1, s32[32,128]{1,0:T(8,128)} %bitcast.8, s32[32,128]{1,0:T(8,128)} %bitcast.9, s32[32,256]{1,0:T(8,128)} %bitcast.7, bf16[84,2048]{1,0:T(8,128)(2,1)} %target_hbm.1, ...), custom_call_target="tpu_custom_call" | custom-call | flops 12000000000 | bytes 6000000 | tf_op jit(solution)/shard_map/pallas_call | solution.py:712
  61.3 2.1 %shard_map.177 = (bf16[1,256,512]{2,1,0:T(8,128)(2,1)}, f32[512,512]{1,0:T(8,128)}) custom-call(bf16[256,512]{1,0:T(8,128)(2,1)} %get-tuple-element.4.mesh_hbm, bf16[2,512,256]{2,1,0:T(8,128)(2,1)} %get-tuple-element.5.grad_hbm), custom_call_target="tpu_custom_call" | custom-call | tf_op jit(solution)/shard_map/pallas_call | solution.py:729

commit v6 on v5

--- a/solution.py
+++ b/solution.py
@@ -307,14 +307,30 @@
     def send_plane(i, carry):
         z = lax.rem(mz + plane_offset(i), PLANES)
         pick_plane(z)
-        copy_plane(z)
+
+        @pl.when(core == 0)
+        def _():
+            copy_plane(z)
+
+        return carry
+
+    def late_plane(i, carry):
+        copy_plane(lax.rem(mz + plane_offset(i), PLANES))
         return carry
 
     with jax.named_scope("send_columns"):
         pick_plane(lax.rem(mz + 1, PLANES))
         pl.semaphore_wait(barrier, REGIONS - 1 + len(beyond) + 1)
-        copy_plane(lax.rem(mz + 1, PLANES))
+
+        @pl.when(core == 0)
+        def _():
+            copy_plane(lax.rem(mz + 1, PLANES))
+
         lax.fori_loop(1, PLANES, send_plane, 0)
+
+        @pl.when(core == 1)
+        def _():
+            lax.fori_loop(0, PLANES, late_plane, 0)
 
     with jax.named_scope("tables"):
         ld_esrc.wait()

time: 63.5 us -> 63.1 us (level)
  no operation moved by 1% of the time
where the time goes in v6:
time: 63.1 us; the launch traced here: 63 us
  Pallas kernels  61.7 us (98%)
  between operations  1.29 us (2%)
    pallas_call x1, Pallas kernels, body(): pl.pallas_call(kernel, out_shape=(jax.ShapeDtypeStruct((NODES, D), BF), j...  59.6 us
    pallas_call x1, Pallas kernels, body(): pl.pallas_call(widen, out_shape=(jax.ShapeDtypeStruct((1, NODES, D), BF),...  2.08 us

profile of v6, /device:TPU:1, one launch (start us, length us, event | category | flops | bytes accessed | tf_op | source)
XLA Modules:
  0.0 63.0 jit_solution(16297885740501842502)
XLA Ops:
  1.3 59.6 %shard_map.176 = (bf16[256,512]{1,0:T(8,128)(2,1)}, bf16[2,512,256]{2,1,0:T(8,128)(2,1)}) custom-call(s32[1,1]{1,0:T(1,128)} %bitcast.6.level_ref, s32[1,32,128]{2,1,0:T(8,128)} %send_hbm.1, s32[32,128]{1,0:T(8,128)} %bitcast.8, s32[32,128]{1,0:T(8,128)} %bitcast.9, s32[32,256]{1,0:T(8,128)} %bitcast.7, bf16[84,2048]{1,0:T(8,128)(2,1)} %target_hbm.1, ...), custom_call_target="tpu_custom_call" | custom-call | flops 12000000000 | bytes 6000000 | tf_op jit(solution)/shard_map/pallas_call | solution.py:728
  60.9 2.1 %shard_map.177 = (bf16[1,256,512]{2,1,0:T(8,128)(2,1)}, f32[512,512]{1,0:T(8,128)}) custom-call(bf16[256,512]{1,0:T(8,128)(2,1)} %get-tuple-element.4.mesh_hbm, bf16[2,512,256]{2,1,0:T(8,128)(2,1)} %get-tuple-element.5.grad_hbm), custom_call_target="tpu_custom_call" | custom-call | tf_op jit(solution)/shard_map/pallas_call | solution.py:745
